TPU v7x, 128 devices: a whole 4x4x4 slice. The times are simulated.
128 devices in a mesh: gx: 8 (over x, y_lo), gy: 16 (over z, y_hi, core).
Axes of the slice: x: 4, y: 4 (y_hi: 2, y_lo: 2; y = y_hi * 2 + y_lo), z: 4, core: 2. Of those that a mesh axis runs over, the one named last changes fastest.
Arguments:
- activation: bfloat16 [128, 64, 128, 128], P(None, 'gx', 'gy'), may hold values from -6 to 6
- cotangent: bfloat16 [128, 64, 128, 128], P(None, 'gx', 'gy'), may hold values from -6 to 6
- in_factor: bfloat16 [128, 32], replicated, may hold values from -0.5 to 0.5
- core: bfloat16 [3, 3, 3, 32, 32], replicated, may hold values from -0.21875 to 0.21875
- out_factor: bfloat16 [128, 32], replicated, may hold values from -1 to 1
Outputs:
- grad_activation: bfloat16 [128, 64, 128, 128], P(None, 'gx', 'gy')
- grad_in_factor: float32 [128, 32], replicated
- grad_core: float32 [3, 3, 3, 32, 32], replicated
- grad_out_factor: float32 [128, 32], replicated
All inputs are finite; a program needn't handle non-finite values.
Results may differ from a plain program's by a relative error of at most 0.0065.
Values may be sent and summed in bfloat16 or wider, within the bound.
A program may use at most 128 MiB of HBM per device.

v0:
```python
import jax
import jax.numpy as jnp
from jax import lax
from jax.sharding import PartitionSpec as P


def extended(x, sides, width):
    for axis, dim in sides:
        peers, length = (lax.axis_size(axis), x.shape[dim])
        up = [(i, (i + 1) % peers) for i in range(peers - 1)]
        down = [(j, i) for i, j in up]
        last = lax.slice_in_dim(x, length - width, length, axis=dim)
        first = lax.slice_in_dim(x, 0, width, axis=dim)
        before = lax.ppermute(last, axis, up)
        after = lax.ppermute(first, axis, down)
        x = jnp.concatenate([before, x, after], axis=dim)
    return x


def shifted(x, axis, by):
    peers = lax.axis_size(axis)
    pairs = [(i, i + by) for i in range(peers) if 0 <= i + by < peers]
    return lax.ppermute(x, axis, pairs)


def take_z(field, offset):
    size = field.shape[-1]
    if offset == 0:
        return field
    widths = [(0, 0)] * (field.ndim - 1)
    if offset > 0:
        return jnp.pad(field[..., offset:], widths + [(0, offset)])
    return jnp.pad(field[..., : size + offset], widths + [(-offset, 0)])


def z_stack(field, sign):
    return jnp.concatenate([take_z(field, sign * (e - 1)) for e in range(3)], axis=0)


def shards(activation, cotangent, in_factor, core, out_factor):
    cells_x = activation.shape[1]
    cells_y = activation.shape[2]
    planes = activation.shape[3]
    rank_in = in_factor.shape[1]
    rank_out = out_factor.shape[1]
    reduced = jnp.einsum(
        "ci,cxyz->ixyz", in_factor, activation, preferred_element_type=jnp.float32
    ).astype(jnp.bfloat16)
    grad_mixed = jnp.einsum(
        "co,cxyz->oxyz", out_factor, cotangent, preferred_element_type=jnp.float32
    ).astype(jnp.bfloat16)
    padded = extended(reduced, (("gx", 1), ("gy", 2)), 1)
    stacked = z_stack(padded, 1)
    forward_core = core.transpose(0, 1, 3, 2, 4).reshape(3, 3, rank_out, 3 * rank_in)
    total = jnp.zeros((rank_out, cells_x, cells_y, planes), jnp.float32)
    for a in range(3):
        for b in range(3):
            window = stacked[:, a : a + cells_x, b : b + cells_y]
            total = total + jnp.einsum(
                "ok,kxyz->oxyz", forward_core[a, b], window, preferred_element_type=jnp.float32
            )
    mixed = total.astype(jnp.bfloat16)
    grad_out_factor = jnp.einsum(
        "cxyz,oxyz->co", cotangent, mixed, preferred_element_type=jnp.float32
    )
    core_terms = []
    for a in range(3):
        for b in range(3):
            window = stacked[:, a : a + cells_x, b : b + cells_y]
            core_terms.append(
                jnp.einsum("oxyz,kxyz->ok", grad_mixed, window, preferred_element_type=jnp.float32)
            )
    grad_core = jnp.stack(core_terms).reshape(3, 3, rank_out, 3, rank_in).transpose(0, 1, 3, 2, 4)
    widened = jnp.zeros((rank_in, cells_x + 2, cells_y + 2, planes), jnp.float32)
    for a in range(3):
        for b in range(3):
            contrib = jnp.einsum(
                "ok,oxyz->kxyz", forward_core[a, b], grad_mixed, preferred_element_type=jnp.float32
            )
            parts = contrib.reshape(3, rank_in, cells_x, cells_y, planes)
            moved = take_z(parts[0], 1) + parts[1] + take_z(parts[2], -1)
            widened = widened.at[:, a : a + cells_x, b : b + cells_y].add(moved)
    inner = widened[:, 1 : cells_x + 1]
    for step_by, source, target in ((-1, 0, cells_x - 1), (1, cells_x + 1, 0)):
        arrived = shifted(widened[:, source], "gx", step_by)
        inner = inner.at[:, target].add(arrived)
    owned = inner[:, :, 1 : cells_y + 1]
    for step_by, source, target in ((-1, 0, cells_y - 1), (1, cells_y + 1, 0)):
        arrived = shifted(inner[:, :, source], "gy", step_by)
        owned = owned.at[:, :, target].add(arrived)
    grad_reduced = owned.astype(jnp.bfloat16)
    grad_in_factor = jnp.einsum(
        "cxyz,ixyz->ci", activation, grad_reduced, preferred_element_type=jnp.float32
    )
    grad_activation = jnp.einsum(
        "ci,ixyz->cxyz", in_factor, grad_reduced, preferred_element_type=jnp.float32
    ).astype(jnp.bfloat16)
    grad_in_factor, grad_core, grad_out_factor = lax.psum(
        (grad_in_factor, grad_core, grad_out_factor), ("gx", "gy")
    )
    return (grad_activation, grad_in_factor, grad_core, grad_out_factor)


def solution(mesh):
    placed = (P(None, "gx", "gy", None), P(None, "gx", "gy", None), P(), P(), P())
    return jax.shard_map(
        shards,
        mesh=mesh,
        in_specs=placed,
        out_specs=(P(None, "gx", "gy", None), P(), P(), P()),
        check_vma=False,
    )
```

profile of v0, /device:TPU:1, one launch (start us, length us, event | category | flops | bytes accessed | tf_op | source)
XLA Modules:
  0.0 316.9 jit_solution(16311022407064301922)
XLA Ops:
  7.2 3.2 %fusion.78 = bf16[32,8,8,128]{3,0,2,1:T(8,128)(2,1)S(1)} fusion(bf16[128,8,8,128]{3,2,1,0:T(8,128)(2,1)} %param.31, bf16[128,32]{0,1:T(8,128)(2,1)} %param.33), kind=kOutput, calls=%fused_computation.71 | convolution fusion | flops 67371008 | bytes 2629632 | tf_op jit(solution)/shard_map/ci,cxyz->ixyz/dot_general | solution.py:46
  10.4 4.0 %collective-permute-start.4 = (bf16[32,1,8,128]{3,0,2,1:T(8,128)(2,1)S(1)}, bf16[32,1,8,128]{3,0,2,1:T(8,128)(2,1)S(1)}, u32[]{:S(2)}, u32[]{:S(2)}) collective-permute-start(bf16[32,1,8,128]{3,0,2,1:T(8,128)(2,1)S(1)} %get-tuple-element.196), channel_id=1, source_target_pairs={{0,16},{16,32},{32,48},{48,64},{64,80},{80,96},{96,112},{1,17},{17... | collective-permute-start | bytes 196616 | tf_op jit(solution)/shard_map/ppermute | solution.py:14
  14.5 1.3 collective-permute-start.5
  16.2 1.4 fusion.75
  23.0 1.3 fusion.188
  24.4 1.7 fusion.187
  26.6 1.7 fusion.186
  28.9 1.4 fusion.185
  32.2 1.6 fusion.167
  35.0 3.2 %fusion.166 = f32[32,10,10,128]{3,0,2,1:T(8,128)S(1)} fusion(f32[32,10,10,128]{3,0,2,1:T(8,128)S(1)} %scatter-add.44, s32[]{:T(128)} %bitcast.7, s32[]{:T(128)} %bitcast.8, f32[96,8,8,128]{3,0,2,1:T(8,128)S(1)} %convolution_bitcast_fusion.7, f32[32,8,8,127]{3,0,2,1:T(8,128)} %get-tuple-element.185, f32[32,8,8,127]{3,0,2,1:T(8,128)S(1)} %copy-done.8), kind=kLoop, calls=%fused_computation.123 | loop fusion | flops 786432 | bytes 5234696 | tf_op jit(solution)/shard_map/scatter-add | solution.py:82
  38.3 2.5 fusion.144
  44.0 5.4 %collective-permute-start.6 = (bf16[32,10,1,128]{3,0,2,1:T(8,128)(2,1)S(1)}, bf16[32,10,1,128]{3,0,2,1:T(8,128)(2,1)S(1)}, u32[]{:S(2)}, u32[]{:S(2)}) collective-permute-start(bf16[32,10,1,128]{3,0,2,1:T(8,128)(2,1)S(1)} %get-tuple-element.194), channel_id=1, source_target_pairs={{0,1},{1,2},{2,3},{3,4},{4,5},{5,6},{6,7},{7,8},{8,9},{9,10},{10,1... | collective-permute-start | bytes 245768 | tf_op jit(solution)/shard_map/ppermute | solution.py:14
  49.4 1.9 collective-permute-start.7
  52.1 1.3 collective-permute-start
  53.4 5.0 %collective-permute-start.1 = (f32[32,10,128]{2,0,1:T(8,128)}, f32[32,10,128]{2,0,1:T(8,128)}, u32[]{:S(2)}, u32[]{:S(2)}) collective-permute-start(f32[32,10,128]{2,0,1:T(8,128)} %get-tuple-element.188), channel_id=1, source_target_pairs={{0,16},{16,32},{32,48},{48,64},{64,80},{80,96},{96,112},{1,17},{17... | collective-permute-start | bytes 491528 | tf_op jit(solution)/shard_map/ppermute | solution.py:23
  58.3 1.2 slice.784
  60.0 0.9 fusion.2
  61.0 1.5 fusion.87
  62.4 1.3 fusion.12
  63.7 1.4 fusion.16
  65.1 1.3 fusion.20
  66.4 1.3 fusion.24
  67.8 1.4 fusion.28
  69.2 1.3 fusion.32
  70.5 1.3 fusion.36
  71.8 1.2 fusion.93
  73.1 1.3 fusion.99
  74.3 1.2 fusion.105
  75.6 1.2 fusion.111
  76.8 1.2 fusion.117
  78.0 1.2 fusion.123
  79.3 1.2 fusion.129
  80.5 1.2 fusion.135
  81.8 2.1 reshape.587
  83.9 2.8 fusion.40
  86.7 1.0 fusion.173
  87.7 1.0 fusion.172
  88.7 0.8 slice_bitcast_fusion.2
  89.5 1.9 collective-permute-start.2
  91.4 5.7 %fusion.138 = f32[128,32]{0,1:T(8,128)S(1)} fusion(bf16[128,8,8,128]{3,2,1,0:T(8,128)(2,1)S(1)} %copy-done, f32[8,8,128,32]{2,3,1,0:T(8,128)} %fusion.12, f32[8,8,128,32]{2,3,1,0:T(8,128)} %fusion.16, f32[8,8,128,32]{2,3,1,0:T(8,128)} %fusion.20, f32[8,8,128,32]{2,3,1,0:T(8,128)} %fusion.24, f32[8,8,128,32]{2,3,1,0:T(8,128)} %fusion.28, ...), kind=kOutput, calls=%fused_computation.91 | convolution fusion | flops 119799808 | bytes 12083200 | tf_op jit(solution)/shard_map/cxyz,oxyz->co/dot_general | solution.py:63
  98.0 6.2 %collective-permute-start.3 = (f32[32,8,128]{2,0,1:T(8,128)S(1)}, f32[32,8,128]{2,0,1:T(8,128)S(1)}, u32[]{:S(2)}, u32[]{:S(2)}) collective-permute-start(f32[32,8,128]{2,0,1:T(8,128)S(1)} %copy-done.10), channel_id=1, source_target_pairs={{0,1},{1,2},{2,3},{3,4},{4,5},{5,6},{6,7},{7,8},{8,9},{9,10},{10,1... | collective-permute-start | bytes 393224 | tf_op jit(solution)/shard_map/ppermute | solution.py:23
  104.2 130.0 %all-reduce.24.cloned.1.call-done = f32[3,3,3,32,32]{4,2,3,1,0:T(4,128)} async-done(((f32[3,3,3,32,32]{4,2,3,1,0:T(4,128)}), f32[3,3,3,32,32]{4,2,3,1,0:T(4,128)}) %all-reduce.24.cloned.1.call-update) | async-done | bytes 110608 | tf_op jit(solution)/shard_map/psum | solution.py:98
  234.2 1.9 copy.32
  236.1 1.0 fusion.176
  237.1 2.9 fusion.141
  240.0 2.1 convert_bitcast_fusion
  242.1 4.1 %copy.31 = bf16[128,8,8,128]{3,2,1,0:T(8,128)(2,1)} copy(bf16[128,8,8,128]{0,3,2,1:T(8,128)(2,1)} %convert_bitcast_fusion) | data formatting | bytes 4194304
  246.2 63.8 %all-reduce.21 = (f32[128,32]{0,1:T(8,128)}, f32[128,32]{0,1:T(8,128)}) all-reduce(f32[128,32]{0,1:T(8,128)S(1)} %fusion.141, f32[128,32]{0,1:T(8,128)S(1)} %fusion.138), channel_id=1, replica_groups=mesh['gx'=8,'gy'=16] {'gx','gy'}, use_global_device_ids=true, to_apply=%region_1.2 | all-reduce | flops 8192 | bytes 65536 | tf_op jit(solution)/shard_map/psum | solution.py:98
  (74 shorter events, 15.4 us)
Async XLA Ops:
  7.2 9.0 %copy-start = (bf16[128,8,8,128]{3,2,1,0:T(8,128)(2,1)S(1)}, bf16[128,8,8,128]{3,2,1,0:T(8,128)(2,1)}, u32[]{:S(2)}) copy-start(bf16[128,8,8,128]{3,2,1,0:T(8,128)(2,1)} %param.32) | copy-start | bytes 6291460
  7.2 8.6 %copy-start.9 = (bf16[3,3,3,32,32]{4,3,2,1,0:T(8,128)(2,1)S(1)}, bf16[3,3,3,32,32]{4,3,2,1,0:T(8,128)(2,1)}, u32[]{:S(2)}) copy-start(bf16[3,3,3,32,32]{4,3,2,1,0:T(8,128)(2,1)} %param.34) | copy-start | bytes 165892
  7.2 9.0 %copy-start.12 = (bf16[128,32]{0,1:T(8,128)(2,1)S(1)}, bf16[128,32]{0,1:T(8,128)(2,1)}, u32[]{:S(2)}) copy-start(bf16[128,32]{0,1:T(8,128)(2,1)} %param.35) | copy-start | bytes 24580
  7.2 227.0 %all-reduce.24.cloned.1.call-start = ((), (), s32[]{:S(2)}) async-start(), calls=%async_computation | async-start | bytes 1179648 | tf_op jit(solution)/shard_map/psum | solution.py:98
  10.4 33.5 %collective-permute-start.4 = (bf16[32,1,8,128]{3,0,2,1:T(8,128)(2,1)S(1)}, bf16[32,1,8,128]{3,0,2,1:T(8,128)(2,1)S(1)}, u32[]{:S(2)}, u32[]{:S(2)}) collective-permute-start(bf16[32,1,8,128]{3,0,2,1:T(8,128)(2,1)S(1)} %get-tuple-element.196), channel_id=1, source_target_pairs={{0,16},{16,32},{32,48},{48,64},{64,80},{80,96},{96,112},{1,17},{17... | collective-permute-start | bytes 196616 | tf_op jit(solution)/shard_map/ppermute | solution.py:14
  14.5 29.5 %collective-permute-start.5 = (bf16[32,1,8,128]{3,0,2,1:T(8,128)(2,1)S(1)}, bf16[32,1,8,128]{3,0,2,1:T(8,128)(2,1)S(1)}, u32[]{:S(2)}, u32[]{:S(2)}) collective-permute-start(bf16[32,1,8,128]{3,0,2,1:T(8,128)(2,1)S(1)} %get-tuple-element.197), channel_id=1, source_target_pairs={{16,0},{32,16},{48,32},{64,48},{80,64},{96,80},{112,96},{17,1},{33... | collective-permute-start | bytes 196616 | tf_op jit(solution)/shard_map/ppermute | solution.py:15
  32.2 1.8 copy-start.13
  33.8 1.2 copy-start.8
  35.0 3.2 %copy-start.6 = (f32[32,8,8,127]{3,0,2,1:T(8,128)S(1)}, f32[32,8,8,127]{3,0,2,1:T(8,128)}, u32[]{:S(2)}) copy-start(f32[32,8,8,127]{3,0,2,1:T(8,128)} %get-tuple-element.182) | copy-start | bytes 3121156
  35.0 3.2 %copy-start.7 = (f32[32,8,8,127]{3,0,2,1:T(8,128)S(1)}, f32[32,8,8,127]{3,0,2,1:T(8,128)}, u32[]{:S(2)}) copy-start(f32[32,8,8,127]{3,0,2,1:T(8,128)} %get-tuple-element.183) | copy-start | bytes 3121156
  38.3 2.6 copy-start.5
  44.0 15.7 %copy-start.2 = (f32[32,10,10,128]{3,0,2,1:T(8,128)}, f32[32,10,10,128]{3,0,2,1:T(8,128)S(1)}, u32[]{:S(2)}) copy-start(f32[32,10,10,128]{3,0,2,1:T(8,128)S(1)} %fusion.147) | copy-start | bytes 4915204
  44.0 15.5 %collective-permute-start.6 = (bf16[32,10,1,128]{3,0,2,1:T(8,128)(2,1)S(1)}, bf16[32,10,1,128]{3,0,2,1:T(8,128)(2,1)S(1)}, u32[]{:S(2)}, u32[]{:S(2)}) collective-permute-start(bf16[32,10,1,128]{3,0,2,1:T(8,128)(2,1)S(1)} %get-tuple-element.194), channel_id=1, source_target_pairs={{0,1},{1,2},{2,3},{3,4},{4,5},{5,6},{6,7},{7,8},{8,9},{9,10},{10,1... | collective-permute-start | bytes 245768 | tf_op jit(solution)/shard_map/ppermute | solution.py:14
  49.4 10.1 %collective-permute-start.7 = (bf16[32,10,1,128]{3,0,2,1:T(8,128)(2,1)S(1)}, bf16[32,10,1,128]{3,0,2,1:T(8,128)(2,1)S(1)}, u32[]{:S(2)}, u32[]{:S(2)}) collective-permute-start(bf16[32,10,1,128]{3,0,2,1:T(8,128)(2,1)S(1)} %get-tuple-element.195), channel_id=1, source_target_pairs={{1,0},{2,1},{3,2},{4,3},{5,4},{6,5},{7,6},{8,7},{9,8},{10,9},{11,1... | collective-permute-start | bytes 245768 | tf_op jit(solution)/shard_map/ppermute | solution.py:15
  52.1 34.6 %collective-permute-start = (f32[32,10,128]{2,0,1:T(8,128)}, f32[32,10,128]{2,0,1:T(8,128)}, u32[]{:S(2)}, u32[]{:S(2)}) collective-permute-start(f32[32,10,128]{2,0,1:T(8,128)} %get-tuple-element.189), channel_id=1, source_target_pairs={{16,0},{32,16},{48,32},{64,48},{80,64},{96,80},{112,96},{17,1},{33... | collective-permute-start | bytes 491528 | tf_op jit(solution)/shard_map/ppermute | solution.py:23
  53.4 34.3 %collective-permute-start.1 = (f32[32,10,128]{2,0,1:T(8,128)}, f32[32,10,128]{2,0,1:T(8,128)}, u32[]{:S(2)}, u32[]{:S(2)}) collective-permute-start(f32[32,10,128]{2,0,1:T(8,128)} %get-tuple-element.188), channel_id=1, source_target_pairs={{0,16},{16,32},{32,48},{48,64},{64,80},{80,96},{96,112},{1,17},{17... | collective-permute-start | bytes 491528 | tf_op jit(solution)/shard_map/ppermute | solution.py:23
  60.9 19.6 %copy-start.1 = (bf16[96,10,10,128]{3,0,2,1:T(8,128)(2,1)}, bf16[96,10,10,128]{3,0,2,1:T(8,128)(2,1)S(1)}, u32[]{:S(2)}) copy-start(bf16[96,10,10,128]{3,0,2,1:T(8,128)(2,1)S(1)} %fusion.2) | copy-start | bytes 7372804
  81.8 4.9 %copy-start.3 = (f32[32,8,10,128]{3,0,2,1:T(8,128)S(1)}, f32[32,8,10,128]{3,0,2,1:T(8,128)}, u32[]{:S(2)}) copy-start(f32[32,8,10,128]{3,0,2,1:T(8,128)} %slice.784) | copy-start | bytes 3932164
  88.7 8.5 %copy-start.4 = (f32[32,8,10,128]{3,0,2,1:T(8,128)}, f32[32,8,10,128]{3,0,2,1:T(8,128)S(1)}, u32[]{:S(2)}) copy-start(f32[32,8,10,128]{3,0,2,1:T(8,128)S(1)} %fusion.172) | copy-start | bytes 3932164
  89.5 146.6 %collective-permute-start.2 = (f32[32,8,128]{2,0,1:T(8,128)}, f32[32,8,128]{2,0,1:T(8,128)}, u32[]{:S(2)}, u32[]{:S(2)}) collective-permute-start(f32[32,8,128]{2,0,1:T(8,128)} %get-tuple-element.191), channel_id=1, source_target_pairs={{1,0},{2,1},{3,2},{4,3},{5,4},{6,5},{7,6},{8,7},{9,8},{10,9},{11,1... | collective-permute-start | bytes 393224 | tf_op jit(solution)/shard_map/ppermute | solution.py:23
  97.1 0.9 copy-start.10
  98.0 142.0 %copy-start.11 = (bf16[128,32]{0,1:T(8,128)(2,1)S(1)}, bf16[128,32]{0,1:T(8,128)(2,1)}, u32[]{:S(2)}) copy-start(bf16[128,32]{0,1:T(8,128)(2,1)} %param.33) | copy-start | bytes 24580
  98.0 139.0 %collective-permute-start.3 = (f32[32,8,128]{2,0,1:T(8,128)S(1)}, f32[32,8,128]{2,0,1:T(8,128)S(1)}, u32[]{:S(2)}, u32[]{:S(2)}) collective-permute-start(f32[32,8,128]{2,0,1:T(8,128)S(1)} %copy-done.10), channel_id=1, source_target_pairs={{0,1},{1,2},{2,3},{3,4},{4,5},{5,6},{6,7},{7,8},{8,9},{9,10},{10,1... | collective-permute-start | bytes 393224 | tf_op jit(solution)/shard_map/ppermute | solution.py:23
Sparse Core Ops, SparseCore 0:
  84.0 150.1 all-reduce.23
where the time goes:
time: 318 us; the launch traced here: 317 us
  waiting for transfers between devices  130 us (41%)
  blocking collectives  63.8 us (20%)
  matrix products  44.3 us (14%)
  starting transfers between devices  27 us (8%)
  local copies, waits for them, and re-layouts  22 us (7%)
  other arithmetic  15.2 us (5%)
  between operations  14.6 us (5%)
    psum x1, waiting for transfers between devices, shards(): lax.psum((grad_in_factor, grad_core, grad_out_factor), ('gx', 'gy'))  130 us
    psum x1, blocking collectives, shards(): lax.psum((grad_in_factor, grad_core, grad_out_factor), ('gx', 'gy'))  63.8 us
    ppermute x4, starting transfers between devices, shifted(): return lax.ppermute(x, axis, pairs)  14.3 us
    dot_general x8, matrix products, shards(): jnp.einsum('ok,kxyz->oxyz', forward_core[a, b], window, preferred_element...  12.2 us
    dot_general x9, matrix products, shards(): jnp.einsum('oxyz,kxyz->ok', grad_mixed, window, preferred_element_type=jn...  11.4 us
    ppermute x2, starting transfers between devices, extended(): before = lax.ppermute(last, axis, up)  9.4 us
    scatter-add x8, other arithmetic, shards(): widened = widened.at[:, a:a + cells_x, b:b + cells_y].add(moved)  8.86 us
    slice x9, local copies, waits for them, and re-layouts, take_z(): return jnp.pad(field[..., offset:], widths + [(0, offset)])  7.97 us
  transfers between devices with their start and end apart: 9, of which 1 were waited for; matrix products, arithmetic and copies ran while one was open for 21% of the time, Pallas kernels for 0%

commit v1 on v0

v1 whole, which is shorter than its diff:
```python
import functools

import jax
import jax.numpy as jnp
from jax import lax
from jax.experimental import pallas as pl
from jax.experimental.pallas import tpu as pltpu
from jax.sharding import PartitionSpec as P

MESH = pl.DeviceIdType.MESH
F32 = jnp.float32
BF16 = jnp.bfloat16
WAYS = ((1, 0), (-1, 0), (0, 1), (0, -1), (1, 1), (1, -1), (-1, 1), (-1, -1))
R = 32
ROWS = 11


def mm(a, b):
    return lax.dot_general(a, b, (((1,), (0,)), ((), ())), preferred_element_type=F32)


def mm_nt(a, b):
    return lax.dot_general(a, b, (((1,), (1,)), ((), ())), preferred_element_type=F32)


def iota(shape, dim):
    return lax.broadcasted_iota(jnp.int32, shape, dim)


def z_copies(v):
    lane = iota(v.shape, 1)
    less = jnp.where(lane == 0, 0.0, pltpu.roll(v, 1, 1))
    more = jnp.where(lane == 127, 0.0, pltpu.roll(v, 127, 1))
    return less.astype(BF16), v.astype(BF16), more.astype(BF16)


def spread(factor_t):
    repeat = (iota((8 * R, R), 0) % R == iota((8 * R, R), 1)).astype(BF16)
    rows = mm(repeat, factor_t).astype(BF16)
    widen = (iota((128, 1024), 1) // 8 == iota((128, 1024), 0)).astype(BF16)
    wide = mm(rows, widen)
    keep = iota((8 * R, 1024), 1) % 8 == iota((8 * R, 1024), 0) // R
    return jnp.where(keep, wide, 0.0).astype(BF16)


def spread_t(factor_t):
    lift = (iota((1024, 128), 0) // 8 == iota((1024, 128), 1)).astype(BF16)
    repeat = (iota((8 * R, R), 0) % R == iota((8 * R, R), 1)).astype(BF16)
    rows = mm(repeat, factor_t).astype(BF16)
    tall = mm_nt(lift, rows)
    keep = iota((1024, 8 * R), 0) % 8 == iota((1024, 8 * R), 1) // R
    return jnp.where(keep, tall, 0.0).astype(BF16)


def fold(g):
    keep = iota(g.shape, 0) % 8 == iota(g.shape, 1) // R
    g = jnp.where(keep, g, 0.0)
    g = g[:, :128] + g[:, 128:]
    g = jnp.sum(g.reshape(128, 8, 128), axis=1)
    g = g + pltpu.roll(g, 64, 1)
    g = g + pltpu.roll(g, 32, 1)
    return jnp.transpose(g)[:R]


def kernel(dims, act, cot, inf, core, outf, gact, gcore, gin, gout,
           act_v, cot_v, a2, c2, xs_r, xs_g, red, gmu, hx_r, hx_g, hy_r, hy_g, hxs, hys,
           t_s, w32, w_f, w_b, y32, wk_i, wk_o, wk_t, acc_m, acc_b, part, rs_recv, y_buf, y_recv, fin, gact_v,
           in_sem, out_sem, send_sem, recv_sem, ar_sem):
    n_gx, n_gy = dims
    n_x, n_z = n_gx // 2, n_gy // 4
    group = n_x * n_z * 2
    per = R // group
    gx, gy = lax.axis_index("gx"), lax.axis_index("gy")
    x, y_lo = gx // 2, gx % 2
    z, y_hi, cr = gy // 4, (gy // 2) % 2, gy % 2
    me = (x * n_z + z) * 2 + cr
    my_y = y_hi * 2 + y_lo

    def by_group(j):
        return (j // (2 * n_z)) * 2 + y_lo, ((j // 2) % n_z) * 4 + y_hi * 2 + j % 2

    def by_y(j):
        return x * 2 + j % 2, z * 4 + (j // 2) * 2 + cr

    pairs = ((0, 7), (1, 2), (3, 4), (5, 6))
    loads = []
    for n, (src, dst) in enumerate(((cot, cot_v), (act, act_v))):
        mine = []
        for p in pairs:
            for xx in p:
                c = pltpu.make_async_copy(src.at[:, xx], dst.at[:, xx], in_sem.at[n, xx])
                c.start()
                mine.append(c)
        loads.append(mine)

    for ref in (hx_r, hx_g, hy_r, hy_g):
        ref[...] = jnp.zeros(ref.shape, BF16)
    barrier = pltpu.get_barrier_semaphore()
    for dx, dy in WAYS:
        pl.semaphore_signal(barrier, inc=1, device_id=((gx + dx + n_gx) % n_gx, (gy + dy + n_gy) % n_gy), device_id_type=MESH)

    def greet_group(k, c):
        pl.semaphore_signal(barrier, inc=1, device_id=by_group((me + k) % group), device_id_type=MESH)
        return c

    lax.fori_loop(1, group, greet_group, 0)
    for k in range(1, 4):
        pl.semaphore_signal(barrier, inc=1, device_id=by_y((my_y + k) % 4), device_id_type=MESH)

    wk_o[...] = spread(outf[...])
    wk_i[...] = spread(inf[...])
    for ref in (xs_r, red):
        ref[:, 0:128] = jnp.zeros((ref.shape[0], 128), BF16)
        ref[:, 1152:1280] = jnp.zeros((ref.shape[0], 128), BF16)
    xs_g[:, 0:128] = jnp.zeros((768, 128), BF16)
    xs_g[:, 1152:1280] = jnp.zeros((768, 128), BF16)
    red[0:32, 128:1152] = jnp.zeros((32, 1024), BF16)
    red[288:320, 128:1152] = jnp.zeros((32, 1024), BF16)

    def inside(gxx, gyy):
        return (gxx >= 0) & (gxx < n_gx) & (gyy >= 0) & (gyy < n_gy)

    def send_copy(field, way):
        dx, dy = WAYS[way]
        src, row0, lane0, hx, hy = (gmu, 0, 0, hx_g, hy_g) if field == 0 else (red, 32, 128, hx_r, hy_r)
        edge_x = lane0 + (896 if dx > 0 else 0)
        edge_y = row0 + (224 if dy > 0 else 0)
        if dy == 0:
            s = src.at[pl.ds(row0, 256), pl.ds(edge_x, 128)]
            d = hx.at[0 if dx > 0 else 1, pl.ds(32, 256), :]
        elif dx == 0:
            s = src.at[pl.ds(edge_y, 32), pl.ds(lane0, 1024)]
            d = hy.at[0 if dy > 0 else 1, :, pl.ds(128, 1024)]
        else:
            s = src.at[pl.ds(edge_y, 32), pl.ds(edge_x, 128)]
            d = hy.at[0 if dy > 0 else 1, :, pl.ds(0 if dx > 0 else 1152, 128)]
        return pltpu.make_async_remote_copy(
            src_ref=s, dst_ref=d, send_sem=send_sem.at[field, way], recv_sem=recv_sem.at[field, way],
            device_id=((gx + dx + n_gx) % n_gx, (gy + dy + n_gy) % n_gy), device_id_type=MESH)

    def send(field, way):
        dx, dy = WAYS[way]

        @pl.when(inside(gx + dx, gy + dy))
        def _():
            send_copy(field, way).start()

    def arrive(field, way):
        dx, dy = WAYS[way]

        @pl.when(inside(gx - dx, gy - dy))
        def _():
            send_copy(field, way).wait_recv()

    def sent(field, way):
        dx, dy = WAYS[way]

        @pl.when(inside(gx + dx, gy + dy))
        def _():
            send_copy(field, way).wait_send()

    for field, (raw, flat, wk, xs) in enumerate(((cot_v, c2, wk_o, xs_g), (act_v, a2, wk_i, xs_r))):
        for n, p in enumerate(pairs):
            for side, xx in enumerate(p):
                loads[field][2 * n + side].wait()
                flat[:, xx * 128:xx * 128 + 128] = raw[:, xx].astype(F32).reshape(1024, 128).astype(BF16)
            both = jnp.concatenate([flat[:, xx * 128:xx * 128 + 128] for xx in p], axis=1)
            r = mm(wk[...], both)
            for side, xx in enumerate(p):
                v = r[:, side * 128:side * 128 + 128].astype(BF16).astype(F32)
                copies = z_copies(v)
                if field == 0:
                    gmu[:, xx * 128:xx * 128 + 128] = copies[1]
                else:
                    red[32:288, xx * 128 + 128:xx * 128 + 256] = copies[1]
                for yy in range(8):
                    for e in range(3):
                        xs[yy * 96 + e * 32:yy * 96 + e * 32 + 32, xx * 128 + 128:xx * 128 + 256] = copies[e][yy * 32:yy * 32 + 32]
            if n == 0:
                if field == 0:
                    pl.semaphore_wait(barrier, 8 + group - 1 + 3)
                send(field, 0)
                send(field, 1)
        for way in range(2, 8):
            send(field, way)

    eye = (iota((R, R), 0) == iota((R, R), 1)).astype(BF16)
    for n, w in enumerate((w_f, w_b)):
        w32[...] = jnp.zeros(w32.shape, F32)
        for a in range(3):
            if n == 0:
                for b in range(3):
                    for e in range(3):
                        t_s[:, (b * 3 + e) * 32:(b * 3 + e) * 32 + 32] = core[a, b, e].astype(F32)
            else:
                blocks = [core[2 - a, 2 - b, 2 - e] for b in range(3) for e in range(3)]
                t_s[:, 0:288] = mm_nt(eye, jnp.concatenate(blocks, axis=0))
            for yy in range(8):
                lo = 96 if yy == 0 else 0
                hi = 192 if yy == 7 else 288
                at = a * 768 + 96 * (yy - 1) + lo
                w32[yy * 32:yy * 32 + 32, at:at + hi - lo] = t_s[:, lo:hi]
            y32[n, 0, :, a * 96:a * 96 + 96] = t_s[:, 0:96]
            y32[n, 1, :, a * 96:a * 96 + 96] = t_s[:, 192:288]
        w[...] = w32[...].astype(BF16)
    wk_t[...] = spread_t(inf[...])

    for w, xs, acc in ((w_b, xs_g, acc_b), (w_f, xs_r, acc_m)):
        for t in range(4):
            k = jnp.concatenate([xs[:, (a + 2 * t) * 128:(a + 2 * t) * 128 + 256] for a in range(3)], axis=0)
            acc[:, t * 256:t * 256 + 256] = mm(w[...], k)
    g = jnp.zeros((192, 384), F32)
    for p in range(4):
        k = jnp.concatenate([red[64 * p:64 * p + 128, a * 128:a * 128 + 1024] for a in range(3)], axis=0)
        g = g + mm_nt(xs_g[192 * p:192 * p + 192, 128:1152], k)
    for a in range(3):
        second = pltpu.roll(g[96:192, a * 128:a * 128 + 128], 96, 1)
        total = g[0:96, a * 128:a * 128 + 128] + second
        for e in range(3):
            part[:, a * 3 + 2 - e, :] = total[e * 32:e * 32 + 32]

    def correct(n, field, hx, hy, w, acc):
        for way in range(8):
            arrive(field, way)
        for side in range(2):
            copies = z_copies(hx[side, 32:288, :].astype(F32))
            for yy in range(8):
                for e in range(3):
                    hxs[side, yy * 96 + e * 32:yy * 96 + e * 32 + 32, :] = copies[e][yy * 32:yy * 32 + 32]
            for xp in range(10):
                copies = z_copies(hy[side, :, xp * 128:xp * 128 + 128].astype(F32))
                for e in range(3):
                    hys[side, e * 32:e * 32 + 32, xp * 128:xp * 128 + 128] = copies[e]
        for side in range(2):
            at = 896 * side
            acc[:, at:at + 128] += mm(w[:, 1536 * side:1536 * side + 768], hxs[side])
            k = jnp.concatenate([hys[side, :, a * 128:a * 128 + 1024] for a in range(3)], axis=0)
            acc[224 * side:224 * side + 32, :] += mm(y32[n, side, :, 0:288].astype(BF16), k)
        return acc[...].astype(BF16)

    gr = correct(1, 0, hx_g, hy_g, w_b, acc_b)
    part[:, 10, :] = fold(mm_nt(a2[...], gr))
    mixed = correct(0, 1, hx_r, hy_r, w_f, acc_m)
    part[:, 9, :] = fold(mm_nt(c2[...], mixed))

    gx0 = sum(mm_nt(xs_g[192 * p:192 * p + 192, 128:256], hx_r[0, 64 * p:64 * p + 128, :]) for p in range(4))
    gx2 = sum(mm_nt(xs_g[192 * p:192 * p + 192, 1024:1152], hx_r[1, 64 * p:64 * p + 128, :]) for p in range(4))
    gys = []
    for side in range(2):
        k = jnp.concatenate([hy_r[side, :, a * 128:a * 128 + 1024] for a in (0, 1, 2, 2)], axis=0)
        gys.append(mm_nt(xs_g[672 * side:672 * side + 96, 128:1152], k))
    lane = iota((96, 128), 1)
    for a in range(3):
        total = jnp.where(lane < 32, pltpu.roll(gys[0], (128 - 32 * a) % 128, 1), 0.0)
        total = total + jnp.where((lane >= 64) & (lane < 96), pltpu.roll(gys[1], (192 - 32 * a) % 128, 1), 0.0)
        if a != 1:
            gxx = gx0 if a == 0 else gx2
            total = total + gxx[0:96] + pltpu.roll(gxx[96:192], 96, 1)
        for e in range(3):
            part[:, a * 3 + 2 - e, :] += total[e * 32:e * 32 + 32]

    def rs(k):
        j = (me + k) % group
        return pltpu.make_async_remote_copy(
            src_ref=part.at[pl.ds(j * per, per)], dst_ref=rs_recv.at[k - 1], send_sem=ar_sem.at[0], recv_sem=ar_sem.at[1],
            device_id=by_group(j), device_id_type=MESH)

    def start_rs(k, c):
        rs(k).start()
        return c

    lax.fori_loop(1, group, start_rs, 0)

    outs = []
    for t in range(4):
        r = mm(wk_t[...], gr[:, t * 256:t * 256 + 256])
        for side in range(2):
            xx = 2 * t + side
            gact_v[:, xx] = r[:, side * 128:side * 128 + 128].reshape(128, 8, 128).astype(BF16)
        c = pltpu.make_async_copy(gact_v.at[:, pl.ds(2 * t, 2)], gact.at[:, pl.ds(2 * t, 2)], out_sem.at[t])
        c.start()
        outs.append(c)

    def wait_all(ref, sem):
        pltpu.make_async_copy(ref, ref, sem).wait()

    wait_all(rs_recv, ar_sem.at[1])
    y_buf[...] = part[pl.ds(me * per, per)] + jnp.sum(rs_recv[...], axis=0)
    across = []
    for k in range(1, 4):
        c = pltpu.make_async_remote_copy(
            src_ref=y_buf, dst_ref=y_recv.at[k - 1], send_sem=ar_sem.at[2], recv_sem=ar_sem.at[3],
            device_id=by_y((my_y + k) % 4), device_id_type=MESH)
        c.start()
    wait_all(y_recv, ar_sem.at[3])
    s = jnp.zeros(y_buf.shape, F32)
    for j in range(4):
        slot = (my_y - j + 4) % 4
        other = y_recv[jnp.maximum(slot - 1, 0)]
        s = s + jnp.where(slot == 0, y_buf[...], other)
    fin[pl.ds(me * per, per)] = s

    def ag(k):
        j = (me + k) % group
        return pltpu.make_async_remote_copy(
            src_ref=fin.at[pl.ds(me * per, per)], dst_ref=fin.at[pl.ds(me * per, per)], send_sem=ar_sem.at[4], recv_sem=ar_sem.at[5],
            device_id=by_group(j), device_id_type=MESH)

    def start_ag(k, c):
        ag(k).start()
        return c

    lax.fori_loop(1, group, start_ag, 0)
    wait_all(rs_recv, ar_sem.at[5])
    for a in range(3):
        for e in range(3):
            v = fin[:, a * 3 + e, :]
            for b in range(3):
                gcore[a, b, e] = v[:, b * 32:b * 32 + 32]
    gout[...] = fin[:, 9, :]
    gin[...] = fin[:, 10, :]
    wait_all(rs_recv, ar_sem.at[0])
    wait_all(y_recv, ar_sem.at[2])
    wait_all(rs_recv, ar_sem.at[4])
    for field in range(2):
        for way in range(8):
            sent(field, way)
    for c in outs:
        c.wait()


def shards(dims, activation, cotangent, in_factor, core, out_factor):
    n_gx, n_gy = dims
    group = n_gx * n_gy // 4
    per = R // group
    vm = pl.BlockSpec(memory_space=pltpu.VMEM)
    hbm = pl.BlockSpec(memory_space=pl.ANY)
    gact, gcore, gin, gout = pl.pallas_call(
        functools.partial(kernel, dims),
        out_shape=(
            jax.ShapeDtypeStruct(activation.shape, BF16),
            jax.ShapeDtypeStruct((3, 3, 3, R, R), F32),
            jax.ShapeDtypeStruct((R, 128), F32),
            jax.ShapeDtypeStruct((R, 128), F32),
        ),
        in_specs=[hbm, hbm, vm, vm, vm],
        out_specs=(hbm, vm, vm, vm),
        scratch_shapes=[
            pltpu.VMEM((128, 8, 8, 128), BF16),
            pltpu.VMEM((128, 8, 8, 128), BF16),
            pltpu.VMEM((1024, 1024), BF16),
            pltpu.VMEM((1024, 1024), BF16),
            pltpu.VMEM((768, 1280), BF16),
            pltpu.VMEM((768, 1280), BF16),
            pltpu.VMEM((320, 1280), BF16),
            pltpu.VMEM((256, 1024), BF16),
            pltpu.VMEM((2, 320, 128), BF16),
            pltpu.VMEM((2, 320, 128), BF16),
            pltpu.VMEM((2, 32, 1280), BF16),
            pltpu.VMEM((2, 32, 1280), BF16),
            pltpu.VMEM((2, 768, 128), BF16),
            pltpu.VMEM((2, 96, 1280), BF16),
            pltpu.VMEM((32, 384), F32),
            pltpu.VMEM((256, 2304), F32),
            pltpu.VMEM((256, 2304), BF16),
            pltpu.VMEM((256, 2304), BF16),
            pltpu.VMEM((2, 2, 32, 384), F32),
            pltpu.VMEM((256, 1024), BF16),
            pltpu.VMEM((256, 1024), BF16),
            pltpu.VMEM((1024, 256), BF16),
            pltpu.VMEM((256, 1024), F32),
            pltpu.VMEM((256, 1024), F32),
            pltpu.VMEM((R, ROWS, 128), F32),
            pltpu.VMEM((group - 1, per, ROWS, 128), F32),
            pltpu.VMEM((per, ROWS, 128), F32),
            pltpu.VMEM((3, per, ROWS, 128), F32),
            pltpu.VMEM((R, ROWS, 128), F32),
            pltpu.VMEM((128, 8, 8, 128), BF16),
            pltpu.SemaphoreType.DMA((2, 8)),
            pltpu.SemaphoreType.DMA((4,)),
            pltpu.SemaphoreType.DMA((2, 8)),
            pltpu.SemaphoreType.DMA((2, 8)),
            pltpu.SemaphoreType.DMA((6,)),
        ],
        compiler_params=pltpu.CompilerParams(collective_id=0, has_side_effects=True, vmem_limit_bytes=56 * 1024 * 1024),
    )(activation, cotangent, in_factor.T, core, out_factor.T)
    return gact, gin.T, gcore, gout.T


def solution(mesh):
    dims = (mesh.shape["gx"], mesh.shape["gy"])
    placed = (P(None, "gx", "gy", None), P(None, "gx", "gy", None), P(), P(), P())
    return jax.shard_map(
        functools.partial(shards, dims),
        mesh=mesh,
        in_specs=placed,
        out_specs=(P(None, "gx", "gy", None), P(), P(), P()),
        check_vma=False,
    )
```

time: 318 us -> 45.2 us (0.14)
  waiting for transfers between devices: 130 us -> 0 us
  blocking collectives: 63.8 us -> 0 us
  matrix products: 44.3 us -> 0 us
  Pallas kernels: 0 us -> 39.3 us
  starting transfers between devices: 27 us -> 0 us
  local copies, waits for them, and re-layouts: 22 us -> 5.12 us
  other arithmetic: 15.2 us -> 0 us
  between operations: 14.6 us -> 0.67 us
    psum x1 -> x0, waiting for transfers between devices: 130 us -> none  [shards(): lax.psum((grad_in_factor, grad_core, grad_out_factor), ('gx', 'gy'))]
    psum x1 -> x0, blocking collectives: 63.8 us -> none  [shards(): lax.psum((grad_in_factor, grad_core, grad_out_factor), ('gx', 'gy'))]
    dot_general x31 -> x0, matrix products: 44.3 us -> none  [the longest x8 12.2 us: shards(): jnp.einsum('ok,kxyz->oxyz', forward_core[a, b], window, preferred_element...]
    pallas_call x0 -> x1, Pallas kernels: none -> 39.3 us  [shards(): pl.pallas_call(functools.partial(kernel, dims), out_shape=(jax.ShapeDtype...]
    ppermute x8 -> x0, starting transfers between devices: 26.9 us -> none  [the longest x4 14.3 us: shifted(): return lax.ppermute(x, axis, pairs)]
    scatter-add x12 -> x0, other arithmetic: 11.9 us -> none  [the longest x8 8.86 us: shards(): widened = widened.at[:, a:a + cells_x, b:b + cells_y].add(moved)]
    slice x13 -> x0, local copies, waits for them, and re-layouts: 9.53 us -> none  [the longest x9 7.97 us: take_z(): return jnp.pad(field[..., offset:], widths + [(0, offset)])]
    unnamed x31 -> x10, local copies, waits for them, and re-layouts: 7.17 us -> 5.12 us
  transfers between devices with their start and end apart: 9 -> 0, of which waited for: 1 -> 0; matrix products, arithmetic and copies ran while one was open for 21% -> 0% of each run, Pallas kernels for 0% -> 0%
where the time goes in v1:
time: 45.2 us; the launch traced here: 45.1 us
  Pallas kernels  39.3 us (87%)
  local copies, waits for them, and re-layouts  5.12 us (11%)
  between operations  0.67 us (1%)
    pallas_call x1, Pallas kernels, shards(): pl.pallas_call(functools.partial(kernel, dims), out_shape=(jax.ShapeDtype...  39.3 us
    unnamed x10, local copies, waits for them, and re-layouts  5.12 us

profile of v1, /device:TPU:1, one launch (start us, length us, event | category | flops | bytes accessed | tf_op | source)
XLA Modules:
  0.0 45.1 jit_solution(7829028174540122810)
XLA Ops:
  0.6 39.3 %shard_map.84 = (bf16[128,8,8,128]{3,2,1,0:T(8,128)(2,1)}, f32[3,3,3,32,32]{4,3,2,1,0:T(8,128)}, f32[32,128]{1,0:T(8,128)}, f32[32,128]{1,0:T(8,128)}) custom-call(bf16[128,8,8,128]{3,2,1,0:T(8,128)(2,1)} %act.1, bf16[128,8,8,128]{3,2,1,0:T(8,128)(2,1)} %cot.1, bf16[32,128]{1,0:T(8,128)(2,1)} %bitcast.6, bf16[3,3,3,32,32]{4,3,2,1,0:T(8,128)(2,1)} %core.1, ...), custom_call_target="tpu_custom_call" | custom-call | tf_op jit(solution)/shard_map/pallas_call | solution.py:338
  39.9 0.0 copy-start.2
  39.9 0.0 copy-start
  39.9 0.0 copy-start.1
  40.0 3.1 %copy.13 = bf16[128,8,8,128]{3,2,1,0:T(8,128)(2,1)} copy(bf16[128,8,8,128]{3,2,1,0:T(8,128)(2,1)} %get-tuple-element.16) | data formatting | bytes 4194304
  43.1 0.0 copy-done.2
  43.1 0.6 %copy.14 = f32[128,32]{0,1:T(8,128)} copy(f32[128,32]{0,1:T(8,128)S(1)} %bitcast.5) | data formatting | bytes 32768
  43.7 0.0 copy-done
  43.7 0.8 %copy.15 = f32[3,3,3,32,32]{4,3,2,1,0:T(8,128)} copy(f32[3,3,3,32,32]{4,3,2,1,0:T(8,128)S(1)} %copy-done) | data formatting | bytes 221184
  44.5 0.0 copy-done.1
  44.5 0.6 %copy.16 = f32[128,32]{0,1:T(8,128)} copy(f32[128,32]{0,1:T(8,128)S(1)} %bitcast.4) | data formatting | bytes 32768
Async XLA Ops:
  39.9 3.2 %copy-start.2 = (f32[32,128]{1,0:T(8,128)S(1)}, f32[32,128]{1,0:T(8,128)}, u32[]{:S(2)}) copy-start(f32[32,128]{1,0:T(8,128)} %get-tuple-element.9) | copy-start | bytes 49156
  39.9 3.8 %copy-start = (f32[3,3,3,32,32]{4,3,2,1,0:T(8,128)S(1)}, f32[3,3,3,32,32]{4,3,2,1,0:T(8,128)}, u32[]{:S(2)}) copy-start(f32[3,3,3,32,32]{4,3,2,1,0:T(8,128)} %get-tuple-element.18) | copy-start | bytes 331780
  39.9 4.5 %copy-start.1 = (f32[32,128]{1,0:T(8,128)S(1)}, f32[32,128]{1,0:T(8,128)}, u32[]{:S(2)}) copy-start(f32[32,128]{1,0:T(8,128)} %get-tuple-element.11) | copy-start | bytes 49156

commit v2 on v1

--- a/solution.py
+++ b/solution.py
@@ -12,7 +12,8 @@
 BF16 = jnp.bfloat16
 WAYS = ((1, 0), (-1, 0), (0, 1), (0, -1), (1, 1), (1, -1), (-1, 1), (-1, -1))
 R = 32
-ROWS = 11
+ROWS = 9
+HALF = R // 2
 
 
 def mm(a, b):
@@ -62,10 +63,10 @@
     return jnp.transpose(g)[:R]
 
 
-def kernel(dims, act, cot, inf, core, outf, gact, gcore, gin, gout,
+def kernel(dims, act, cot, inf, core, outf, gact_v, gcore, gin, gout,
            act_v, cot_v, a2, c2, xs_r, xs_g, red, gmu, hx_r, hx_g, hy_r, hy_g, hxs, hys,
-           t_s, w32, w_f, w_b, y32, wk_i, wk_o, wk_t, acc_m, acc_b, part, rs_recv, y_buf, y_recv, fin, gact_v,
-           in_sem, out_sem, send_sem, recv_sem, ar_sem):
+           t_s, w32, w_f, w_b, y32, wk_i, wk_o, wk_t, acc_m, acc_b, own, part, rs_recv, y_recv, fin, part2, c_recv, xz_recv, y2_recv,
+           in_sem, send_sem, recv_sem, ar_sem, f_sem):
     n_gx, n_gy = dims
     n_x, n_z = n_gx // 2, n_gy // 4
     group = n_x * n_z * 2
@@ -86,11 +87,10 @@
     loads = []
     for n, (src, dst) in enumerate(((cot, cot_v), (act, act_v))):
         mine = []
-        for p in pairs:
-            for xx in p:
-                c = pltpu.make_async_copy(src.at[:, xx], dst.at[:, xx], in_sem.at[n, xx])
-                c.start()
-                mine.append(c)
+        for k, xx in enumerate((pl.ds(0, 1), pl.ds(7, 1), pl.ds(1, 6))):
+            c = pltpu.make_async_copy(src.at[:, xx], dst.at[:, xx], in_sem.at[n, k])
+            c.start()
+            mine.append(c)
         loads.append(mine)
 
     for ref in (hx_r, hx_g, hy_r, hy_g):
@@ -127,7 +127,7 @@
         edge_y = row0 + (224 if dy > 0 else 0)
         if dy == 0:
             s = src.at[pl.ds(row0, 256), pl.ds(edge_x, 128)]
-            d = hx.at[0 if dx > 0 else 1, pl.ds(32, 256), :]
+            d = hx.at[0 if dx > 0 else 1]
         elif dx == 0:
             s = src.at[pl.ds(edge_y, 32), pl.ds(lane0, 1024)]
             d = hy.at[0 if dy > 0 else 1, :, pl.ds(128, 1024)]
@@ -161,8 +161,9 @@
 
     for field, (raw, flat, wk, xs) in enumerate(((cot_v, c2, wk_o, xs_g), (act_v, a2, wk_i, xs_r))):
         for n, p in enumerate(pairs):
-            for side, xx in enumerate(p):
-                loads[field][2 * n + side].wait()
+            for c in loads[field][0:2] if n == 0 else loads[field][2:3] if n == 1 else ():
+                c.wait()
+            for xx in p:
                 flat[:, xx * 128:xx * 128 + 128] = raw[:, xx].astype(F32).reshape(1024, 128).astype(BF16)
             both = jnp.concatenate([flat[:, xx * 128:xx * 128 + 128] for xx in p], axis=1)
             r = mm(wk[...], both)
@@ -215,15 +216,13 @@
         g = g + mm_nt(xs_g[192 * p:192 * p + 192, 128:1152], k)
     for a in range(3):
         second = pltpu.roll(g[96:192, a * 128:a * 128 + 128], 96, 1)
-        total = g[0:96, a * 128:a * 128 + 128] + second
-        for e in range(3):
-            part[:, a * 3 + 2 - e, :] = total[e * 32:e * 32 + 32]
-
-    def correct(n, field, hx, hy, w, acc):
+        own[a] = g[0:96, a * 128:a * 128 + 128] + second
+
+    def halo_copies(field, hx, hy):
         for way in range(8):
             arrive(field, way)
         for side in range(2):
-            copies = z_copies(hx[side, 32:288, :].astype(F32))
+            copies = z_copies(hx[side].astype(F32))
             for yy in range(8):
                 for e in range(3):
                     hxs[side, yy * 96 + e * 32:yy * 96 + e * 32 + 32, :] = copies[e][yy * 32:yy * 32 + 32]
@@ -231,6 +230,8 @@
                 copies = z_copies(hy[side, :, xp * 128:xp * 128 + 128].astype(F32))
                 for e in range(3):
                     hys[side, e * 32:e * 32 + 32, xp * 128:xp * 128 + 128] = copies[e]
+
+    def correct(n, w, acc):
         for side in range(2):
             at = 896 * side
             acc[:, at:at + 128] += mm(w[:, 1536 * side:1536 * side + 768], hxs[side])
@@ -238,94 +239,138 @@
             acc[224 * side:224 * side + 32, :] += mm(y32[n, side, :, 0:288].astype(BF16), k)
         return acc[...].astype(BF16)
 
-    gr = correct(1, 0, hx_g, hy_g, w_b, acc_b)
-    part[:, 10, :] = fold(mm_nt(a2[...], gr))
-    mixed = correct(0, 1, hx_r, hy_r, w_f, acc_m)
-    part[:, 9, :] = fold(mm_nt(c2[...], mixed))
-
-    gx0 = sum(mm_nt(xs_g[192 * p:192 * p + 192, 128:256], hx_r[0, 64 * p:64 * p + 128, :]) for p in range(4))
-    gx2 = sum(mm_nt(xs_g[192 * p:192 * p + 192, 1024:1152], hx_r[1, 64 * p:64 * p + 128, :]) for p in range(4))
-    gys = []
+    halo_copies(0, hx_g, hy_g)
+    g_x = []
     for side in range(2):
-        k = jnp.concatenate([hy_r[side, :, a * 128:a * 128 + 1024] for a in (0, 1, 2, 2)], axis=0)
-        gys.append(mm_nt(xs_g[672 * side:672 * side + 96, 128:1152], k))
-    lane = iota((96, 128), 1)
+        lanes = pl.ds(128 + 896 * side, 128)
+        g_x.append(sum(mm_nt(hxs[side, 192 * p:192 * p + 192, :], red[64 * p:64 * p + 128, lanes]) for p in range(4)))
+    g_y = jnp.zeros((288, 128), F32)
+    for side in range(2):
+        k = jnp.concatenate([hys[side, :, (2 - a) * 128:(2 - a) * 128 + 1024] for a in range(3)], axis=0)
+        row = red[32 + 224 * side:64 + 224 * side, 128:1152]
+        none = jnp.zeros_like(row)
+        row = jnp.concatenate([none, none, row, none] if side == 0 else [row, none, none, none], axis=0)
+        g_y = g_y + mm_nt(k, row)
     for a in range(3):
-        total = jnp.where(lane < 32, pltpu.roll(gys[0], (128 - 32 * a) % 128, 1), 0.0)
-        total = total + jnp.where((lane >= 64) & (lane < 96), pltpu.roll(gys[1], (192 - 32 * a) % 128, 1), 0.0)
+        total = own[a] + g_y[a * 96:a * 96 + 96]
         if a != 1:
-            gxx = gx0 if a == 0 else gx2
+            gxx = g_x[0] if a == 2 else g_x[1]
             total = total + gxx[0:96] + pltpu.roll(gxx[96:192], 96, 1)
         for e in range(3):
-            part[:, a * 3 + 2 - e, :] += total[e * 32:e * 32 + 32]
-
-    def rs(k):
+            part[:, a * 3 + 2 - e, :] = total[e * 32:e * 32 + 32]
+
+    def wait_all(ref, sem):
+        pltpu.make_async_copy(ref, ref, sem).wait()
+
+    def start_y(buf, n):
+        for k in range(1, 4):
+            pltpu.make_async_remote_copy(
+                src_ref=buf.at[my_y], dst_ref=buf.at[my_y], send_sem=ar_sem.at[n], recv_sem=ar_sem.at[n + 1],
+                device_id=by_y((my_y + k) % 4), device_id_type=MESH).start()
+
+    def start_rs(k, c):
         j = (me + k) % group
+        pltpu.make_async_remote_copy(
+            src_ref=part.at[pl.ds(j * per, per)], dst_ref=rs_recv.at[k - 1], send_sem=ar_sem.at[0], recv_sem=ar_sem.at[1],
+            device_id=by_group(j), device_id_type=MESH).start()
+        return c
+
+    def start_ag(k, c):
+        pltpu.make_async_remote_copy(
+            src_ref=fin.at[pl.ds(me * per, per)], dst_ref=fin.at[pl.ds(me * per, per)], send_sem=ar_sem.at[4], recv_sem=ar_sem.at[5],
+            device_id=by_group((me + k) % group), device_id_type=MESH).start()
+        return c
+
+    other = (gx, gy + 1 - 2 * cr)
+    mine, theirs = pl.ds(pl.multiple_of(cr * HALF, HALF), HALF), pl.ds(pl.multiple_of((1 - cr) * HALF, HALF), HALF)
+    plane = n_x * n_z
+    at = x * n_z + z
+    results = (gin, gout)
+
+    def to_core(n):
         return pltpu.make_async_remote_copy(
-            src_ref=part.at[pl.ds(j * per, per)], dst_ref=rs_recv.at[k - 1], send_sem=ar_sem.at[0], recv_sem=ar_sem.at[1],
-            device_id=by_group(j), device_id_type=MESH)
-
-    def start_rs(k, c):
-        rs(k).start()
-        return c
+            src_ref=part2.at[n, theirs], dst_ref=c_recv.at[n], send_sem=f_sem.at[n, 0], recv_sem=f_sem.at[n, 1],
+            device_id=other, device_id_type=MESH)
+
+    def over_xz(n):
+        to_core(n).wait_recv()
+        xz_recv[n, at] = part2[n, mine] + c_recv[n]
+
+        def start_xz(k, c):
+            j = (at + k) % plane
+            pltpu.make_async_remote_copy(
+                src_ref=xz_recv.at[n, at], dst_ref=xz_recv.at[n, at], send_sem=f_sem.at[n, 2], recv_sem=f_sem.at[n, 3],
+                device_id=((j // n_z) * 2 + y_lo, (j % n_z) * 4 + y_hi * 2 + cr), device_id_type=MESH).start()
+            return c
+
+        lax.fori_loop(1, plane, start_xz, 0)
+
+    def over_y(n):
+        wait_all(xz_recv.at[n, pl.ds(0, plane - 1)], f_sem.at[n, 3])
+        y2_recv[n, my_y] = jnp.sum(xz_recv[n], axis=0)
+        start_y(y2_recv.at[n], 6 + 2 * n)
+
+    def swap(n):
+        return pltpu.make_async_remote_copy(
+            src_ref=results[n].at[mine], dst_ref=results[n].at[mine], send_sem=f_sem.at[n, 4], recv_sem=f_sem.at[n, 5],
+            device_id=other, device_id_type=MESH)
+
+    def back(n):
+        wait_all(y2_recv.at[n, pl.ds(0, 3)], ar_sem.at[7 + 2 * n])
+        results[n][mine] = jnp.sum(y2_recv[n], axis=0)
+        swap(n).start()
 
     lax.fori_loop(1, group, start_rs, 0)
-
-    outs = []
+    gr = correct(1, w_b, acc_b)
+    part2[0] = fold(mm_nt(a2[...], gr))
+    to_core(0).start()
     for t in range(4):
         r = mm(wk_t[...], gr[:, t * 256:t * 256 + 256])
         for side in range(2):
-            xx = 2 * t + side
-            gact_v[:, xx] = r[:, side * 128:side * 128 + 128].reshape(128, 8, 128).astype(BF16)
-        c = pltpu.make_async_copy(gact_v.at[:, pl.ds(2 * t, 2)], gact.at[:, pl.ds(2 * t, 2)], out_sem.at[t])
-        c.start()
-        outs.append(c)
-
-    def wait_all(ref, sem):
-        pltpu.make_async_copy(ref, ref, sem).wait()
+            gact_v[:, 2 * t + side] = r[:, side * 128:side * 128 + 128].reshape(128, 8, 128).astype(BF16)
+    over_xz(0)
+
+    halo_copies(1, hx_r, hy_r)
+    mixed = correct(0, w_f, acc_m)
+    part2[1] = fold(mm_nt(c2[...], mixed))
+    to_core(1).start()
 
     wait_all(rs_recv, ar_sem.at[1])
-    y_buf[...] = part[pl.ds(me * per, per)] + jnp.sum(rs_recv[...], axis=0)
-    across = []
-    for k in range(1, 4):
-        c = pltpu.make_async_remote_copy(
-            src_ref=y_buf, dst_ref=y_recv.at[k - 1], send_sem=ar_sem.at[2], recv_sem=ar_sem.at[3],
-            device_id=by_y((my_y + k) % 4), device_id_type=MESH)
-        c.start()
-    wait_all(y_recv, ar_sem.at[3])
-    s = jnp.zeros(y_buf.shape, F32)
-    for j in range(4):
-        slot = (my_y - j + 4) % 4
-        other = y_recv[jnp.maximum(slot - 1, 0)]
-        s = s + jnp.where(slot == 0, y_buf[...], other)
-    fin[pl.ds(me * per, per)] = s
-
-    def ag(k):
-        j = (me + k) % group
-        return pltpu.make_async_remote_copy(
-            src_ref=fin.at[pl.ds(me * per, per)], dst_ref=fin.at[pl.ds(me * per, per)], send_sem=ar_sem.at[4], recv_sem=ar_sem.at[5],
-            device_id=by_group(j), device_id_type=MESH)
-
-    def start_ag(k, c):
-        ag(k).start()
-        return c
-
+    y_recv[my_y] = part[pl.ds(me * per, per)] + jnp.sum(rs_recv[...], axis=0)
+    start_y(y_recv, 2)
+    over_xz(1)
+    over_y(0)
+    wait_all(y_recv.at[pl.ds(0, 3)], ar_sem.at[3])
+    fin[pl.ds(me * per, per)] = jnp.sum(y_recv[...], axis=0)
     lax.fori_loop(1, group, start_ag, 0)
+    over_y(1)
+    back(0)
+    back(1)
     wait_all(rs_recv, ar_sem.at[5])
     for a in range(3):
         for e in range(3):
             v = fin[:, a * 3 + e, :]
             for b in range(3):
                 gcore[a, b, e] = v[:, b * 32:b * 32 + 32]
-    gout[...] = fin[:, 9, :]
-    gin[...] = fin[:, 10, :]
     wait_all(rs_recv, ar_sem.at[0])
-    wait_all(y_recv, ar_sem.at[2])
+    wait_all(y_recv.at[pl.ds(0, 3)], ar_sem.at[2])
     wait_all(rs_recv, ar_sem.at[4])
+    for n in range(2):
+        swap(n).wait_recv()
+        to_core(n).wait_send()
+        wait_all(xz_recv.at[n, pl.ds(0, plane - 1)], f_sem.at[n, 2])
+        wait_all(y2_recv.at[n, pl.ds(0, 3)], ar_sem.at[6 + 2 * n])
+        swap(n).wait_send()
     for field in range(2):
         for way in range(8):
             sent(field, way)
-    for c in outs:
+
+
+def finish(*refs):
+    copies = [pltpu.make_async_copy(refs[n], refs[n + 4], refs[8].at[n]) for n in range(4)]
+    for c in copies:
+        c.start()
+    for c in copies:
         c.wait()
 
 
@@ -335,16 +380,16 @@
     per = R // group
     vm = pl.BlockSpec(memory_space=pltpu.VMEM)
     hbm = pl.BlockSpec(memory_space=pl.ANY)
-    gact, gcore, gin, gout = pl.pallas_call(
+    held = pl.pallas_call(
         functools.partial(kernel, dims),
         out_shape=(
-            jax.ShapeDtypeStruct(activation.shape, BF16),
-            jax.ShapeDtypeStruct((3, 3, 3, R, R), F32),
-            jax.ShapeDtypeStruct((R, 128), F32),
-            jax.ShapeDtypeStruct((R, 128), F32),
+            pltpu.VMEM(activation.shape, BF16),
+            pltpu.VMEM((3, 3, 3, R, R), F32),
+            pltpu.VMEM((R, 128), F32),
+            pltpu.VMEM((R, 128), F32),
         ),
         in_specs=[hbm, hbm, vm, vm, vm],
-        out_specs=(hbm, vm, vm, vm),
+        out_specs=(vm, vm, vm, vm),
         scratch_shapes=[
             pltpu.VMEM((128, 8, 8, 128), BF16),
             pltpu.VMEM((128, 8, 8, 128), BF16),
@@ -354,8 +399,8 @@
             pltpu.VMEM((768, 1280), BF16),
             pltpu.VMEM((320, 1280), BF16),
             pltpu.VMEM((256, 1024), BF16),
-            pltpu.VMEM((2, 320, 128), BF16),
-            pltpu.VMEM((2, 320, 128), BF16),
+            pltpu.VMEM((2, 256, 128), BF16),
+            pltpu.VMEM((2, 256, 128), BF16),
             pltpu.VMEM((2, 32, 1280), BF16),
             pltpu.VMEM((2, 32, 1280), BF16),
             pltpu.VMEM((2, 768, 128), BF16),
@@ -370,20 +415,36 @@
             pltpu.VMEM((1024, 256), BF16),
             pltpu.VMEM((256, 1024), F32),
             pltpu.VMEM((256, 1024), F32),
+            pltpu.VMEM((3, 96, 128), F32),
             pltpu.VMEM((R, ROWS, 128), F32),
             pltpu.VMEM((group - 1, per, ROWS, 128), F32),
-            pltpu.VMEM((per, ROWS, 128), F32),
-            pltpu.VMEM((3, per, ROWS, 128), F32),
+            pltpu.VMEM((4, per, ROWS, 128), F32),
             pltpu.VMEM((R, ROWS, 128), F32),
-            pltpu.VMEM((128, 8, 8, 128), BF16),
-            pltpu.SemaphoreType.DMA((2, 8)),
-            pltpu.SemaphoreType.DMA((4,)),
+            pltpu.VMEM((2, R, 128), F32),
+            pltpu.VMEM((2, HALF, 128), F32),
+            pltpu.VMEM((2, group // 2, HALF, 128), F32),
+            pltpu.VMEM((2, 4, HALF, 128), F32),
+            pltpu.SemaphoreType.DMA((2, 3)),
             pltpu.SemaphoreType.DMA((2, 8)),
             pltpu.SemaphoreType.DMA((2, 8)),
-            pltpu.SemaphoreType.DMA((6,)),
+            pltpu.SemaphoreType.DMA((10,)),
+            pltpu.SemaphoreType.DMA((2, 6)),
         ],
-        compiler_params=pltpu.CompilerParams(collective_id=0, has_side_effects=True, vmem_limit_bytes=56 * 1024 * 1024),
+        compiler_params=pltpu.CompilerParams(collective_id=0, has_side_effects=True, vmem_limit_bytes=60 * 1024 * 1024),
     )(activation, cotangent, in_factor.T, core, out_factor.T)
+    gact, gcore, gin, gout = pl.pallas_call(
+        finish,
+        out_shape=(
+            jax.ShapeDtypeStruct(activation.shape, BF16),
+            jax.ShapeDtypeStruct((3, 3, 3, R, R), F32),
+            jax.ShapeDtypeStruct((R, 128), F32),
+            jax.ShapeDtypeStruct((R, 128), F32),
+        ),
+        in_specs=[vm] * 4,
+        out_specs=(hbm,) * 4,
+        scratch_shapes=[pltpu.SemaphoreType.DMA((4,))],
+        compiler_params=pltpu.CompilerParams(vmem_limit_bytes=24 * 1024 * 1024),
+    )(*held)
     return gact, gin.T, gcore, gout.T
 
 

time: 45.2 us -> 39.9 us (0.88)
  local copies, waits for them, and re-layouts: 5.12 us -> 0 us
    unnamed x10 -> x0, local copies, waits for them, and re-layouts: 5.12 us -> none
    pallas_call x1 -> x2, Pallas kernels: 39.3 us -> 39.1 us  [the longest x1 37.6 us: shards(): pl.pallas_call(functools.partial(kernel, dims), out_shape=(pltpu.VMEM(act...]
where the time goes in v2:
time: 39.9 us; the launch traced here: 39.8 us
  Pallas kernels  39.1 us (98%)
  between operations  0.64 us (2%)
    pallas_call x1, Pallas kernels, shards(): pl.pallas_call(functools.partial(kernel, dims), out_shape=(pltpu.VMEM(act...  37.6 us
    pallas_call x1, Pallas kernels, shards(): pl.pallas_call(finish, out_shape=(jax.ShapeDtypeStruct(activation.shape,...  1.49 us

profile of v2, /device:TPU:1, one launch (start us, length us, event | category | flops | bytes accessed | tf_op | source)
XLA Modules:
  0.0 39.8 jit_solution(7872278000016907929)
XLA Ops:
  0.6 37.6 %shard_map.84 = (bf16[128,8,8,128]{3,2,1,0:T(8,128)(2,1)S(1)}, f32[3,3,3,32,32]{4,3,2,1,0:T(8,128)S(1)}, f32[32,128]{1,0:T(8,128)S(1)}, f32[32,128]{1,0:T(8,128)S(1)}) custom-call(bf16[128,8,8,128]{3,2,1,0:T(8,128)(2,1)} %act.1, bf16[128,8,8,128]{3,2,1,0:T(8,128)(2,1)} %cot.1, bf16[32,128]{1,0:T(8,128)(2,1)} %bitcast.4, bf16[3,3,3,32,32]{4,3,2,1,0:T(8,128)(2,1)} %core.1, ...), custom_call_target="tpu_custom_call" | custom-call | tf_op jit(solution)/shard_map/pallas_call | solution.py:383
  38.3 1.5 %shard_map.85 = (bf16[128,8,8,128]{3,2,1,0:T(8,128)(2,1)}, f32[3,3,3,32,32]{4,3,2,1,0:T(8,128)}, f32[32,128]{1,0:T(8,128)}, f32[32,128]{1,0:T(8,128)}) custom-call(bf16[128,8,8,128]{3,2,1,0:T(8,128)(2,1)S(1)} %get-tuple-element.12.refs_0_, f32[3,3,3,32,32]{4,3,2,1,0:T(8,128)S(1)} %get-tuple-element.13.refs_1_, f32[32,128]{1,0:T(8,128)S(1)} %get-tuple-element.14.refs_2_, ...), custom_call_target="tpu_custom_call" | custom-call | tf_op jit(solution)/shard_map/pallas_call | solution.py:435

commit v3 on v2

--- a/solution.py
+++ b/solution.py
@@ -12,7 +12,7 @@
 BF16 = jnp.bfloat16
 WAYS = ((1, 0), (-1, 0), (0, 1), (0, -1), (1, 1), (1, -1), (-1, 1), (-1, -1))
 R = 32
-ROWS = 9
+ROWS = 10
 HALF = R // 2
 
 
@@ -66,7 +66,7 @@
 def kernel(dims, act, cot, inf, core, outf, gact_v, gcore, gin, gout,
            act_v, cot_v, a2, c2, xs_r, xs_g, red, gmu, hx_r, hx_g, hy_r, hy_g, hxs, hys,
            t_s, w32, w_f, w_b, y32, wk_i, wk_o, wk_t, acc_m, acc_b, own, part, rs_recv, y_recv, fin, part2, c_recv, xz_recv, y2_recv,
-           in_sem, send_sem, recv_sem, ar_sem, f_sem):
+           in_sem, send_sem, recv_sem, ar_sem, f_sem, known):
     n_gx, n_gy = dims
     n_x, n_z = n_gx // 2, n_gy // 4
     group = n_x * n_z * 2
@@ -77,9 +77,6 @@
     me = (x * n_z + z) * 2 + cr
     my_y = y_hi * 2 + y_lo
 
-    def by_group(j):
-        return (j // (2 * n_z)) * 2 + y_lo, ((j // 2) % n_z) * 4 + y_hi * 2 + j % 2
-
     def by_y(j):
         return x * 2 + j % 2, z * 4 + (j // 2) * 2 + cr
 
@@ -96,16 +93,33 @@
     for ref in (hx_r, hx_g, hy_r, hy_g):
         ref[...] = jnp.zeros(ref.shape, BF16)
     barrier = pltpu.get_barrier_semaphore()
-    for dx, dy in WAYS:
-        pl.semaphore_signal(barrier, inc=1, device_id=((gx + dx + n_gx) % n_gx, (gy + dy + n_gy) % n_gy), device_id_type=MESH)
-
-    def greet_group(k, c):
-        pl.semaphore_signal(barrier, inc=1, device_id=by_group((me + k) % group), device_id_type=MESH)
-        return c
-
-    lax.fori_loop(1, group, greet_group, 0)
-    for k in range(1, 4):
-        pl.semaphore_signal(barrier, inc=1, device_id=by_y((my_y + k) % 4), device_id_type=MESH)
+    flip = 1 - 2 * cr
+    has_up, has_down = z < n_z - 1, z > 0
+    first, last = gy == 0, gy == n_gy - 1
+
+    def greet(sem, partners):
+        due = 0
+        for there, dx, dy in partners:
+            who = ((gx + dx + n_gx) % n_gx, gy + dy)
+            if there is True:
+                pl.semaphore_signal(sem, inc=1, device_id=who, device_id_type=MESH)
+                due = due + 1
+            else:
+
+                @pl.when(there)
+                def _():
+                    pl.semaphore_signal(sem, inc=1, device_id=who, device_id_type=MESH)
+
+                due = due + there.astype(jnp.int32)
+        return due
+
+    side_l, side_h = 1 - 2 * y_lo, 2 - 4 * y_hi
+    up, down = jnp.logical_not(last), jnp.logical_not(first)
+    near = [(True if dy == 0 else up if dy > 0 else down, dx, dy) for dx, dy in WAYS]
+    near += [(True, dx, dy) for dx in (2, -2) for dy in (0, flip)]
+    near += [(has_up, 0, 4), (has_up, 0, 4 + flip), (has_down, 0, -4), (has_down, 0, -4 + flip)]
+    near += [(True, side_l, 0), (True, 0, side_h), (True, side_l, side_h)]
+    near_due = greet(barrier, near)
 
     wk_o[...] = spread(outf[...])
     wk_i[...] = spread(inf[...])
@@ -179,11 +193,15 @@
                         xs[yy * 96 + e * 32:yy * 96 + e * 32 + 32, xx * 128 + 128:xx * 128 + 256] = copies[e][yy * 32:yy * 32 + 32]
             if n == 0:
                 if field == 0:
-                    pl.semaphore_wait(barrier, 8 + group - 1 + 3)
+                    pl.semaphore_wait(barrier, near_due)
+                    known_due = greet(known.at[0], [(True, 2, 0), (True, -2, 0), (has_up, 0, 4), (has_down, 0, -4)])
                 send(field, 0)
                 send(field, 1)
         for way in range(2, 8):
             send(field, way)
+
+    pl.semaphore_wait(known.at[0], known_due)
+    known_due = greet(known.at[1], [(z < n_z - 2, 0, 8), (z > 1, 0, -8)])
 
     eye = (iota((R, R), 0) == iota((R, R), 1)).astype(BF16)
     for n, w in enumerate((w_f, w_b)):
@@ -210,6 +228,8 @@
         for t in range(4):
             k = jnp.concatenate([xs[:, (a + 2 * t) * 128:(a + 2 * t) * 128 + 256] for a in range(3)], axis=0)
             acc[:, t * 256:t * 256 + 256] = mm(w[...], k)
+    pl.semaphore_wait(known.at[1], known_due)
+    known_due = greet(known.at[2], [(True, 2, 0), (True, -2, 0), (True, 4, 0)])
     g = jnp.zeros((192, 384), F32)
     for p in range(4):
         k = jnp.concatenate([red[64 * p:64 * p + 128, a * 128:a * 128 + 1024] for a in range(3)], axis=0)
@@ -268,17 +288,29 @@
                 src_ref=buf.at[my_y], dst_ref=buf.at[my_y], send_sem=ar_sem.at[n], recv_sem=ar_sem.at[n + 1],
                 device_id=by_y((my_y + k) % 4), device_id_type=MESH).start()
 
+    def member(k):
+        q = k // 2
+        there_x, there_z, there_c = (x + n_x // 2 + q // n_z) % n_x, (z + n_z // 2 + q) % n_z, (cr + k) % 2
+        return (there_x * n_z + there_z) * 2 + there_c, (there_x * 2 + y_lo, there_z * 4 + y_hi * 2 + there_c)
+
+    myself = 2 * ((n_x // 2) * n_z + n_z // 2)
+
+    def each_member(body):
+        lax.fori_loop(0, myself, body, 0)
+        lax.fori_loop(myself + 1, group, body, 0)
+
     def start_rs(k, c):
-        j = (me + k) % group
+        j, who = member(k)
+        slot = jnp.where(k < myself, k, k - 1)
         pltpu.make_async_remote_copy(
-            src_ref=part.at[pl.ds(j * per, per)], dst_ref=rs_recv.at[k - 1], send_sem=ar_sem.at[0], recv_sem=ar_sem.at[1],
-            device_id=by_group(j), device_id_type=MESH).start()
+            src_ref=part.at[pl.ds(j * per, per)], dst_ref=rs_recv.at[slot], send_sem=ar_sem.at[0], recv_sem=ar_sem.at[1],
+            device_id=who, device_id_type=MESH).start()
         return c
 
     def start_ag(k, c):
         pltpu.make_async_remote_copy(
             src_ref=fin.at[pl.ds(me * per, per)], dst_ref=fin.at[pl.ds(me * per, per)], send_sem=ar_sem.at[4], recv_sem=ar_sem.at[5],
-            device_id=by_group((me + k) % group), device_id_type=MESH).start()
+            device_id=member(k)[1], device_id_type=MESH).start()
         return c
 
     other = (gx, gy + 1 - 2 * cr)
@@ -297,13 +329,14 @@
         xz_recv[n, at] = part2[n, mine] + c_recv[n]
 
         def start_xz(k, c):
-            j = (at + k) % plane
+            there_x, there_z = (x + n_x // 2 + k // n_z) % n_x, (z + n_z // 2 + k) % n_z
             pltpu.make_async_remote_copy(
                 src_ref=xz_recv.at[n, at], dst_ref=xz_recv.at[n, at], send_sem=f_sem.at[n, 2], recv_sem=f_sem.at[n, 3],
-                device_id=((j // n_z) * 2 + y_lo, (j % n_z) * 4 + y_hi * 2 + cr), device_id_type=MESH).start()
+                device_id=(there_x * 2 + y_lo, there_z * 4 + y_hi * 2 + cr), device_id_type=MESH).start()
             return c
 
-        lax.fori_loop(1, plane, start_xz, 0)
+        lax.fori_loop(0, myself // 2, start_xz, 0)
+        lax.fori_loop(myself // 2 + 1, plane, start_xz, 0)
 
     def over_y(n):
         wait_all(xz_recv.at[n, pl.ds(0, plane - 1)], f_sem.at[n, 3])
@@ -320,15 +353,14 @@
         results[n][mine] = jnp.sum(y2_recv[n], axis=0)
         swap(n).start()
 
-    lax.fori_loop(1, group, start_rs, 0)
     gr = correct(1, w_b, acc_b)
-    part2[0] = fold(mm_nt(a2[...], gr))
-    to_core(0).start()
+    part[:, 9, :] = fold(mm_nt(a2[...], gr))
+    pl.semaphore_wait(known.at[2], known_due)
+    each_member(start_rs)
     for t in range(4):
         r = mm(wk_t[...], gr[:, t * 256:t * 256 + 256])
         for side in range(2):
             gact_v[:, 2 * t + side] = r[:, side * 128:side * 128 + 128].reshape(128, 8, 128).astype(BF16)
-    over_xz(0)
 
     halo_copies(1, hx_r, hy_r)
     mixed = correct(0, w_f, acc_m)
@@ -339,12 +371,10 @@
     y_recv[my_y] = part[pl.ds(me * per, per)] + jnp.sum(rs_recv[...], axis=0)
     start_y(y_recv, 2)
     over_xz(1)
-    over_y(0)
     wait_all(y_recv.at[pl.ds(0, 3)], ar_sem.at[3])
     fin[pl.ds(me * per, per)] = jnp.sum(y_recv[...], axis=0)
-    lax.fori_loop(1, group, start_ag, 0)
+    each_member(start_ag)
     over_y(1)
-    back(0)
     back(1)
     wait_all(rs_recv, ar_sem.at[5])
     for a in range(3):
@@ -355,7 +385,8 @@
     wait_all(rs_recv, ar_sem.at[0])
     wait_all(y_recv.at[pl.ds(0, 3)], ar_sem.at[2])
     wait_all(rs_recv, ar_sem.at[4])
-    for n in range(2):
+    gin[...] = fin[:, 9, :]
+    for n in range(1, 2):
         swap(n).wait_recv()
         to_core(n).wait_send()
         wait_all(xz_recv.at[n, pl.ds(0, plane - 1)], f_sem.at[n, 2])
@@ -429,6 +460,7 @@
             pltpu.SemaphoreType.DMA((2, 8)),
             pltpu.SemaphoreType.DMA((10,)),
             pltpu.SemaphoreType.DMA((2, 6)),
+            pltpu.SemaphoreType.REGULAR((3,)),
         ],
         compiler_params=pltpu.CompilerParams(collective_id=0, has_side_effects=True, vmem_limit_bytes=60 * 1024 * 1024),
     )(activation, cotangent, in_factor.T, core, out_factor.T)

time: 39.9 us -> 38 us (0.952)
  Pallas kernels: 39.1 us -> 37.2 us
    pallas_call x1, Pallas kernels: 37.6 us -> 35.7 us  [shards(): pl.pallas_call(functools.partial(kernel, dims), out_shape=(pltpu.VMEM(act...]
where the time goes in v3:
time: 38 us; the launch traced here: 37.8 us
  Pallas kernels  37.2 us (98%)
  between operations  0.64 us (2%)
    pallas_call x1, Pallas kernels, shards(): pl.pallas_call(functools.partial(kernel, dims), out_shape=(pltpu.VMEM(act...  35.7 us
    pallas_call x1, Pallas kernels, shards(): pl.pallas_call(finish, out_shape=(jax.ShapeDtypeStruct(activation.shape,...  1.49 us

profile of v3, /device:TPU:1, one launch (start us, length us, event | category | flops | bytes accessed | tf_op | source)
XLA Modules:
  0.0 37.8 jit_solution(5484725033430628354)
XLA Ops:
  0.6 35.7 %shard_map.84 = (bf16[128,8,8,128]{3,2,1,0:T(8,128)(2,1)S(1)}, f32[3,3,3,32,32]{4,3,2,1,0:T(8,128)S(1)}, f32[32,128]{1,0:T(8,128)S(1)}, f32[32,128]{1,0:T(8,128)S(1)}) custom-call(bf16[128,8,8,128]{3,2,1,0:T(8,128)(2,1)} %act.1, bf16[128,8,8,128]{3,2,1,0:T(8,128)(2,1)} %cot.1, bf16[32,128]{1,0:T(8,128)(2,1)} %bitcast.4, bf16[3,3,3,32,32]{4,3,2,1,0:T(8,128)(2,1)} %core.1, ...), custom_call_target="tpu_custom_call" | custom-call | tf_op jit(solution)/shard_map/pallas_call | solution.py:414
  36.3 1.5 %shard_map.85 = (bf16[128,8,8,128]{3,2,1,0:T(8,128)(2,1)}, f32[3,3,3,32,32]{4,3,2,1,0:T(8,128)}, f32[32,128]{1,0:T(8,128)}, f32[32,128]{1,0:T(8,128)}) custom-call(bf16[128,8,8,128]{3,2,1,0:T(8,128)(2,1)S(1)} %get-tuple-element.12.refs_0_, f32[3,3,3,32,32]{4,3,2,1,0:T(8,128)S(1)} %get-tuple-element.13.refs_1_, f32[32,128]{1,0:T(8,128)S(1)} %get-tuple-element.14.refs_2_, ...), custom_call_target="tpu_custom_call" | custom-call | tf_op jit(solution)/shard_map/pallas_call | solution.py:467

commit v4 on v3

--- a/solution.py
+++ b/solution.py
@@ -118,11 +118,10 @@
     near = [(True if dy == 0 else up if dy > 0 else down, dx, dy) for dx, dy in WAYS]
     near += [(True, dx, dy) for dx in (2, -2) for dy in (0, flip)]
     near += [(has_up, 0, 4), (has_up, 0, 4 + flip), (has_down, 0, -4), (has_down, 0, -4 + flip)]
-    near += [(True, side_l, 0), (True, 0, side_h), (True, side_l, side_h)]
+    near += [(True, dx, dy + dc) for dx, dy in ((side_l, 0), (0, side_h), (side_l, side_h)) for dc in (0, flip)]
     near_due = greet(barrier, near)
 
     wk_o[...] = spread(outf[...])
-    wk_i[...] = spread(inf[...])
     for ref in (xs_r, red):
         ref[:, 0:128] = jnp.zeros((ref.shape[0], 128), BF16)
         ref[:, 1152:1280] = jnp.zeros((ref.shape[0], 128), BF16)
@@ -174,6 +173,8 @@
             send_copy(field, way).wait_send()
 
     for field, (raw, flat, wk, xs) in enumerate(((cot_v, c2, wk_o, xs_g), (act_v, a2, wk_i, xs_r))):
+        if field == 1:
+            wk_i[...] = spread(inf[...])
         for n, p in enumerate(pairs):
             for c in loads[field][0:2] if n == 0 else loads[field][2:3] if n == 1 else ():
                 c.wait()
@@ -340,37 +341,37 @@
 
     def over_y(n):
         wait_all(xz_recv.at[n, pl.ds(0, plane - 1)], f_sem.at[n, 3])
-        y2_recv[n, my_y] = jnp.sum(xz_recv[n], axis=0)
-        start_y(y2_recv.at[n], 6 + 2 * n)
-
-    def swap(n):
-        return pltpu.make_async_remote_copy(
-            src_ref=results[n].at[mine], dst_ref=results[n].at[mine], send_sem=f_sem.at[n, 4], recv_sem=f_sem.at[n, 5],
-            device_id=other, device_id_type=MESH)
+        y2_recv[n, my_y * 2 + cr] = jnp.sum(xz_recv[n], axis=0)
+        for k in range(1, 8):
+            to_y = (my_y + k // 2) % 4
+            who = (x * 2 + to_y % 2, z * 4 + (to_y // 2) * 2 + (cr + k) % 2)
+            pltpu.make_async_remote_copy(
+                src_ref=y2_recv.at[n, my_y * 2 + cr], dst_ref=y2_recv.at[n, my_y * 2 + cr],
+                send_sem=f_sem.at[n, 4], recv_sem=f_sem.at[n, 5], device_id=who, device_id_type=MESH).start()
 
     def back(n):
-        wait_all(y2_recv.at[n, pl.ds(0, 3)], ar_sem.at[7 + 2 * n])
-        results[n][mine] = jnp.sum(y2_recv[n], axis=0)
-        swap(n).start()
+        wait_all(y2_recv.at[n, pl.ds(0, 7)], f_sem.at[n, 5])
+        halves = [(y2_recv[n, c] + y2_recv[n, 2 + c]) + (y2_recv[n, 4 + c] + y2_recv[n, 6 + c]) for c in range(2)]
+        results[n][...] = jnp.concatenate(halves, axis=0)
 
     gr = correct(1, w_b, acc_b)
     part[:, 9, :] = fold(mm_nt(a2[...], gr))
     pl.semaphore_wait(known.at[2], known_due)
     each_member(start_rs)
+
+    halo_copies(1, hx_r, hy_r)
+    mixed = correct(0, w_f, acc_m)
+    part2[1] = fold(mm_nt(c2[...], mixed))
+    to_core(1).start()
     for t in range(4):
         r = mm(wk_t[...], gr[:, t * 256:t * 256 + 256])
         for side in range(2):
             gact_v[:, 2 * t + side] = r[:, side * 128:side * 128 + 128].reshape(128, 8, 128).astype(BF16)
-
-    halo_copies(1, hx_r, hy_r)
-    mixed = correct(0, w_f, acc_m)
-    part2[1] = fold(mm_nt(c2[...], mixed))
-    to_core(1).start()
+    over_xz(1)
 
     wait_all(rs_recv, ar_sem.at[1])
     y_recv[my_y] = part[pl.ds(me * per, per)] + jnp.sum(rs_recv[...], axis=0)
     start_y(y_recv, 2)
-    over_xz(1)
     wait_all(y_recv.at[pl.ds(0, 3)], ar_sem.at[3])
     fin[pl.ds(me * per, per)] = jnp.sum(y_recv[...], axis=0)
     each_member(start_ag)
@@ -387,11 +388,9 @@
     wait_all(rs_recv, ar_sem.at[4])
     gin[...] = fin[:, 9, :]
     for n in range(1, 2):
-        swap(n).wait_recv()
         to_core(n).wait_send()
         wait_all(xz_recv.at[n, pl.ds(0, plane - 1)], f_sem.at[n, 2])
-        wait_all(y2_recv.at[n, pl.ds(0, 3)], ar_sem.at[6 + 2 * n])
-        swap(n).wait_send()
+        wait_all(y2_recv.at[n, pl.ds(0, 7)], f_sem.at[n, 4])
     for field in range(2):
         for way in range(8):
             sent(field, way)
@@ -454,7 +453,7 @@
             pltpu.VMEM((2, R, 128), F32),
             pltpu.VMEM((2, HALF, 128), F32),
             pltpu.VMEM((2, group // 2, HALF, 128), F32),
-            pltpu.VMEM((2, 4, HALF, 128), F32),
+            pltpu.VMEM((2, 8, HALF, 128), F32),
             pltpu.SemaphoreType.DMA((2, 3)),
             pltpu.SemaphoreType.DMA((2, 8)),
             pltpu.SemaphoreType.DMA((2, 8)),

time: 38 us -> 36.5 us (0.961)
  Pallas kernels: 37.2 us -> 35.8 us
    pallas_call x1, Pallas kernels: 35.7 us -> 34.3 us  [shards(): pl.pallas_call(functools.partial(kernel, dims), out_shape=(pltpu.VMEM(act...]
where the time goes in v4:
time: 36.5 us; the launch traced here: 36.4 us
  Pallas kernels  35.8 us (98%)
  between operations  0.64 us (2%)
    pallas_call x1, Pallas kernels, shards(): pl.pallas_call(functools.partial(kernel, dims), out_shape=(pltpu.VMEM(act...  34.3 us
    pallas_call x1, Pallas kernels, shards(): pl.pallas_call(finish, out_shape=(jax.ShapeDtypeStruct(activation.shape,...  1.49 us

profile of v4, /device:TPU:1, one launch (start us, length us, event | category | flops | bytes accessed | tf_op | source)
XLA Modules:
  0.0 36.4 jit_solution(2451134544151804315)
XLA Ops:
  0.6 34.3 %shard_map.84 = (bf16[128,8,8,128]{3,2,1,0:T(8,128)(2,1)S(1)}, f32[3,3,3,32,32]{4,3,2,1,0:T(8,128)S(1)}, f32[32,128]{1,0:T(8,128)S(1)}, f32[32,128]{1,0:T(8,128)S(1)}) custom-call(bf16[128,8,8,128]{3,2,1,0:T(8,128)(2,1)} %act.1, bf16[128,8,8,128]{3,2,1,0:T(8,128)(2,1)} %cot.1, bf16[32,128]{1,0:T(8,128)(2,1)} %bitcast.4, bf16[3,3,3,32,32]{4,3,2,1,0:T(8,128)(2,1)} %core.1, ...), custom_call_target="tpu_custom_call" | custom-call | tf_op jit(solution)/shard_map/pallas_call | solution.py:413
  34.9 1.5 %shard_map.85 = (bf16[128,8,8,128]{3,2,1,0:T(8,128)(2,1)}, f32[3,3,3,32,32]{4,3,2,1,0:T(8,128)}, f32[32,128]{1,0:T(8,128)}, f32[32,128]{1,0:T(8,128)}) custom-call(bf16[128,8,8,128]{3,2,1,0:T(8,128)(2,1)S(1)} %get-tuple-element.12.refs_0_, f32[3,3,3,32,32]{4,3,2,1,0:T(8,128)S(1)} %get-tuple-element.13.refs_1_, f32[32,128]{1,0:T(8,128)S(1)} %get-tuple-element.14.refs_2_, ...), custom_call_target="tpu_custom_call" | custom-call | tf_op jit(solution)/shard_map/pallas_call | solution.py:466

commit v5 on v4

--- a/solution.py
+++ b/solution.py
@@ -30,9 +30,9 @@
 
 def z_copies(v):
     lane = iota(v.shape, 1)
-    less = jnp.where(lane == 0, 0.0, pltpu.roll(v, 1, 1))
-    more = jnp.where(lane == 127, 0.0, pltpu.roll(v, 127, 1))
-    return less.astype(BF16), v.astype(BF16), more.astype(BF16)
+    less = jnp.where(lane == 0, jnp.zeros_like(v), pltpu.roll(v, 1, 1))
+    more = jnp.where(lane == 127, jnp.zeros_like(v), pltpu.roll(v, 127, 1))
+    return less, v, more
 
 
 def spread(factor_t):
@@ -183,7 +183,7 @@
             both = jnp.concatenate([flat[:, xx * 128:xx * 128 + 128] for xx in p], axis=1)
             r = mm(wk[...], both)
             for side, xx in enumerate(p):
-                v = r[:, side * 128:side * 128 + 128].astype(BF16).astype(F32)
+                v = r[:, side * 128:side * 128 + 128].astype(BF16)
                 copies = z_copies(v)
                 if field == 0:
                     gmu[:, xx * 128:xx * 128 + 128] = copies[1]
@@ -205,8 +205,8 @@
     known_due = greet(known.at[1], [(z < n_z - 2, 0, 8), (z > 1, 0, -8)])
 
     eye = (iota((R, R), 0) == iota((R, R), 1)).astype(BF16)
+    w32[...] = jnp.zeros(w32.shape, F32)
     for n, w in enumerate((w_f, w_b)):
-        w32[...] = jnp.zeros(w32.shape, F32)
         for a in range(3):
             if n == 0:
                 for b in range(3):
@@ -239,32 +239,42 @@
         second = pltpu.roll(g[96:192, a * 128:a * 128 + 128], 96, 1)
         own[a] = g[0:96, a * 128:a * 128 + 128] + second
 
-    def halo_copies(field, hx, hy):
-        for way in range(8):
+    def halo_x(field, hx):
+        for way in range(2):
             arrive(field, way)
         for side in range(2):
-            copies = z_copies(hx[side].astype(F32))
+            copies = z_copies(hx[side])
             for yy in range(8):
                 for e in range(3):
                     hxs[side, yy * 96 + e * 32:yy * 96 + e * 32 + 32, :] = copies[e][yy * 32:yy * 32 + 32]
+
+    def halo_y(field, hy):
+        for way in range(2, 8):
+            arrive(field, way)
+        for side in range(2):
             for xp in range(10):
-                copies = z_copies(hy[side, :, xp * 128:xp * 128 + 128].astype(F32))
+                copies = z_copies(hy[side, :, xp * 128:xp * 128 + 128])
                 for e in range(3):
                     hys[side, e * 32:e * 32 + 32, xp * 128:xp * 128 + 128] = copies[e]
 
-    def correct(n, w, acc):
+    def correct_x(w, acc):
         for side in range(2):
             at = 896 * side
             acc[:, at:at + 128] += mm(w[:, 1536 * side:1536 * side + 768], hxs[side])
+
+    def correct_y(n, acc):
+        for side in range(2):
             k = jnp.concatenate([hys[side, :, a * 128:a * 128 + 1024] for a in range(3)], axis=0)
             acc[224 * side:224 * side + 32, :] += mm(y32[n, side, :, 0:288].astype(BF16), k)
         return acc[...].astype(BF16)
 
-    halo_copies(0, hx_g, hy_g)
+    halo_x(0, hx_g)
+    correct_x(w_b, acc_b)
     g_x = []
     for side in range(2):
         lanes = pl.ds(128 + 896 * side, 128)
         g_x.append(sum(mm_nt(hxs[side, 192 * p:192 * p + 192, :], red[64 * p:64 * p + 128, lanes]) for p in range(4)))
+    halo_y(0, hy_g)
     g_y = jnp.zeros((288, 128), F32)
     for side in range(2):
         k = jnp.concatenate([hys[side, :, (2 - a) * 128:(2 - a) * 128 + 1024] for a in range(3)], axis=0)
@@ -354,13 +364,15 @@
         halves = [(y2_recv[n, c] + y2_recv[n, 2 + c]) + (y2_recv[n, 4 + c] + y2_recv[n, 6 + c]) for c in range(2)]
         results[n][...] = jnp.concatenate(halves, axis=0)
 
-    gr = correct(1, w_b, acc_b)
+    gr = correct_y(1, acc_b)
     part[:, 9, :] = fold(mm_nt(a2[...], gr))
     pl.semaphore_wait(known.at[2], known_due)
     each_member(start_rs)
 
-    halo_copies(1, hx_r, hy_r)
-    mixed = correct(0, w_f, acc_m)
+    halo_x(1, hx_r)
+    correct_x(w_f, acc_m)
+    halo_y(1, hy_r)
+    mixed = correct_y(0, acc_m)
     part2[1] = fold(mm_nt(c2[...], mixed))
     to_core(1).start()
     for t in range(4):

time: 36.5 us -> 36.4 us (level)
  no operation moved by 1% of the time
where the time goes in v5:
time: 36.4 us; the launch traced here: 36.2 us
  Pallas kernels  35.6 us (98%)
  between operations  0.64 us (2%)
    pallas_call x1, Pallas kernels, shards(): pl.pallas_call(functools.partial(kernel, dims), out_shape=(pltpu.VMEM(act...  34.1 us
    pallas_call x1, Pallas kernels, shards(): pl.pallas_call(finish, out_shape=(jax.ShapeDtypeStruct(activation.shape,...  1.49 us

profile of v5, /device:TPU:1, one launch (start us, length us, event | category | flops | bytes accessed | tf_op | source)
XLA Modules:
  0.0 36.2 jit_solution(9250714336154071496)
XLA Ops:
  0.6 34.1 %shard_map.84 = (bf16[128,8,8,128]{3,2,1,0:T(8,128)(2,1)S(1)}, f32[3,3,3,32,32]{4,3,2,1,0:T(8,128)S(1)}, f32[32,128]{1,0:T(8,128)S(1)}, f32[32,128]{1,0:T(8,128)S(1)}) custom-call(bf16[128,8,8,128]{3,2,1,0:T(8,128)(2,1)} %act.1, bf16[128,8,8,128]{3,2,1,0:T(8,128)(2,1)} %cot.1, bf16[32,128]{1,0:T(8,128)(2,1)} %bitcast.4, bf16[3,3,3,32,32]{4,3,2,1,0:T(8,128)(2,1)} %core.1, ...), custom_call_target="tpu_custom_call" | custom-call | tf_op jit(solution)/shard_map/pallas_call | solution.py:425
  34.7 1.5 %shard_map.85 = (bf16[128,8,8,128]{3,2,1,0:T(8,128)(2,1)}, f32[3,3,3,32,32]{4,3,2,1,0:T(8,128)}, f32[32,128]{1,0:T(8,128)}, f32[32,128]{1,0:T(8,128)}) custom-call(bf16[128,8,8,128]{3,2,1,0:T(8,128)(2,1)S(1)} %get-tuple-element.12.refs_0_, f32[3,3,3,32,32]{4,3,2,1,0:T(8,128)S(1)} %get-tuple-element.13.refs_1_, f32[32,128]{1,0:T(8,128)S(1)} %get-tuple-element.14.refs_2_, ...), custom_call_target="tpu_custom_call" | custom-call | tf_op jit(solution)/shard_map/pallas_call | solution.py:478

commit v6 on v5

--- a/solution.py
+++ b/solution.py
@@ -409,7 +409,9 @@
 
 
 def finish(*refs):
-    copies = [pltpu.make_async_copy(refs[n], refs[n + 4], refs[8].at[n]) for n in range(4)]
+    copies = [pltpu.make_async_copy(refs[0].at[pl.ds(16 * n, 16)], refs[4].at[pl.ds(16 * n, 16)], refs[8].at[n]) for n in range(8)]
+    copies += [pltpu.make_async_copy(refs[1].at[n], refs[5].at[n], refs[8].at[8 + n]) for n in range(3)]
+    copies += [pltpu.make_async_copy(refs[n], refs[n + 4], refs[8].at[9 + n]) for n in range(2, 4)]
     for c in copies:
         c.start()
     for c in copies:
@@ -485,7 +487,7 @@
         ),
         in_specs=[vm] * 4,
         out_specs=(hbm,) * 4,
-        scratch_shapes=[pltpu.SemaphoreType.DMA((4,))],
+        scratch_shapes=[pltpu.SemaphoreType.DMA((13,))],
         compiler_params=pltpu.CompilerParams(vmem_limit_bytes=24 * 1024 * 1024),
     )(*held)
     return gact, gin.T, gcore, gout.T

time: 36.4 us -> 36.4 us (level)
  no operation moved by 1% of the time
where the time goes in v6:
time: 36.4 us; the launch traced here: 36.3 us
  Pallas kernels  35.7 us (98%)
  between operations  0.64 us (2%)
    pallas_call x1, Pallas kernels, shards(): pl.pallas_call(functools.partial(kernel, dims), out_shape=(pltpu.VMEM(act...  34.1 us
    pallas_call x1, Pallas kernels, shards(): pl.pallas_call(finish, out_shape=(jax.ShapeDtypeStruct(activation.shape,...  1.57 us

profile of v6, /device:TPU:1, one launch (start us, length us, event | category | flops | bytes accessed | tf_op | source)
XLA Modules:
  0.0 36.3 jit_solution(4027943771157628016)
XLA Ops:
  0.6 34.1 %shard_map.84 = (bf16[128,8,8,128]{3,2,1,0:T(8,128)(2,1)S(1)}, f32[3,3,3,32,32]{4,3,2,1,0:T(8,128)S(1)}, f32[32,128]{1,0:T(8,128)S(1)}, f32[32,128]{1,0:T(8,128)S(1)}) custom-call(bf16[128,8,8,128]{3,2,1,0:T(8,128)(2,1)} %act.1, bf16[128,8,8,128]{3,2,1,0:T(8,128)(2,1)} %cot.1, bf16[32,128]{1,0:T(8,128)(2,1)} %bitcast.4, bf16[3,3,3,32,32]{4,3,2,1,0:T(8,128)(2,1)} %core.1, ...), custom_call_target="tpu_custom_call" | custom-call | tf_op jit(solution)/shard_map/pallas_call | solution.py:427
  34.7 1.6 %shard_map.85 = (bf16[128,8,8,128]{3,2,1,0:T(8,128)(2,1)}, f32[3,3,3,32,32]{4,3,2,1,0:T(8,128)}, f32[32,128]{1,0:T(8,128)}, f32[32,128]{1,0:T(8,128)}) custom-call(bf16[128,8,8,128]{3,2,1,0:T(8,128)(2,1)S(1)} %get-tuple-element.12.refs_0_, f32[3,3,3,32,32]{4,3,2,1,0:T(8,128)S(1)} %get-tuple-element.13.refs_1_, f32[32,128]{1,0:T(8,128)S(1)} %get-tuple-element.14.refs_2_, ...), custom_call_target="tpu_custom_call" | custom-call | tf_op jit(solution)/shard_map/pallas_call | solution.py:480
